TPU v7x, 32 devices: a whole 2x2x4 slice. The times are simulated.
32 devices in a mesh: seq: 8 (over z, y), ch: 4 (over x, core).
Axes of the slice: x: 2, y: 2, z: 4, core: 2. Of those that a mesh axis runs over, the one named last changes fastest.
Arguments:
- inputs: bfloat16 [256, 2048], P('ch', 'seq'), may hold values from -6 to 6
- gate_values: bfloat16 [256, 2048], P('ch', 'seq'), may hold values from -6 to 6
- probe_values: bfloat16 [256, 2048], P('ch', 'seq'), may hold values from -6 to 6
- filter_taps: float32 [256, 2048], P('ch', 'seq'), may hold values from -0.125 to 0.125
- member_blocks: int32 [64], P('seq'), may hold values from 0 to 31, as said below
- member_nodes: int32 [64], P('seq'), may hold values from 0 to 8191
- node_place: int32 [8192], replicated, may hold values from 0 to 8191, each once
Outputs:
- position_saliency: float32 [2048], P('seq')
- node_rows: float32 [256, 8192], P('ch', 'seq')
Inputs may be any that keep to these rules, and one draw needn't show every extreme that they name: `member_blocks`: in the g-th aligned group of 8 entries every value lies in g * 4 to (g + 1) * 4 - 1, and each of these values appears in that group at least once. `node_place`: each node appears exactly once.
All inputs are finite; a program needn't handle non-finite values.
Results may differ from a plain program's by a relative error of at most 0.0003.
Values may be sent and summed in bfloat16 or wider, within the bound.
No kernel may reach another device: no remote copies, remote signals or barrier semaphores. Data moves between devices by JAX's collectives and lax.ppermute only.
A program may use at most 64 MiB of HBM per device.

v0:
```python
import functools
import math

import jax
import jax.numpy as jnp
from jax import lax
from jax.experimental import pallas as pl
from jax.experimental.pallas import tpu as pltpu
from jax.sharding import PartitionSpec as P

BLOCK = 64
NODES = 8192
LANES = 128
SUBS = 8
HALF = LANES // 2
FIELD_ROWS = 16
FIELDS = 5
MEMBER_ROW = FIELDS * FIELD_ROWS
PACK_ROWS = MEMBER_ROW + FIELD_ROWS


HIGHEST = lax.Precision.HIGHEST


def iota(shape, dim):
    return lax.broadcasted_iota(jnp.int32, shape, dim)


def halves(vals):
    high = vals.astype(jnp.bfloat16)
    return high, (vals - high.astype(jnp.float32)).astype(jnp.bfloat16)


def pack_kernel(
    blocks_dev, inputs_ref, gate_ref, probe_ref, taps_ref, blocks_ref, nodes_ref, packed_ref
):
    devices = packed_ref.shape[0]

    def put(pair, field, tiles):
        for side in range(2):
            rows = slice(side * SUBS, (side + 1) * SUBS)
            both = jnp.concatenate([tile[rows] for tile in tiles], axis=0)
            place = slice(field * FIELD_ROWS, (field + 1) * FIELD_ROWS)
            packed_ref[2 * pair + side, place, :] = both.astype(jnp.bfloat16)

    for pair in range(devices // 2):
        rows = slice(pair * 2 * SUBS, (pair + 1) * 2 * SUBS)
        columns = [slice(0, LANES), slice(LANES, 2 * LANES)]
        for field, ref in enumerate((inputs_ref, gate_ref, probe_ref)):
            put(pair, field, [ref[rows, cols].astype(jnp.float32) for cols in columns])
        split = [halves(taps_ref[rows, cols]) for cols in columns]
        for term in range(2):
            put(pair, 3 + term, [terms[term].astype(jnp.float32) for terms in split])

    def as_column(row):
        members = row.shape[1]
        same = iota((members, members), 0) == iota((members, members), 1)
        return jnp.sum(jnp.where(same, row, 0).astype(jnp.float32), axis=1, keepdims=True)

    nodes = nodes_ref[...]
    low_lanes = iota((SUBS, LANES), 1) < HALF
    digits = jnp.where(low_lanes, as_column(nodes // LANES), as_column(nodes % LANES))
    places = jnp.broadcast_to(as_column(blocks_ref[...] % blocks_dev), (SUBS, LANES))
    member_rows = jnp.concatenate([digits, places], axis=0).astype(jnp.bfloat16)
    for device in range(devices):
        packed_ref[device, MEMBER_ROW:, :] = member_rows


def half_turn(vals):
    return pltpu.roll(vals, HALF, axis=1)


def saliency_kernel(packed_ref, sums_ref, fields, taps, padded, products):
    devices = packed_ref.shape[0]
    blocks = 2 * devices
    copies = sums_ref.shape[0] // devices
    low_lanes = iota((SUBS, LANES), 1) < HALF
    row_ids = iota((SUBS, LANES), 0)
    below = iota((HALF, LANES), 1) < iota((HALF, LANES), 0)
    for source in range(devices):
        rows = slice(source * SUBS, (source + 1) * SUBS)
        for field in range(3):
            place = slice(field * FIELD_ROWS, (field + 1) * FIELD_ROWS)
            both = packed_ref[source, place, :].astype(jnp.float32)
            fields[field, 0, rows, :] = both[:SUBS]
            fields[field, 1, rows, :] = both[SUBS:]
        high, low = (
            packed_ref[source, (3 + term) * FIELD_ROWS : (4 + term) * FIELD_ROWS, :].astype(
                jnp.float32
            )
            for term in range(2)
        )
        taps[source * FIELD_ROWS : (source + 1) * FIELD_ROWS, :] = high + low
    zeros = jnp.zeros((SUBS, LANES), jnp.float32)
    for channel in range(SUBS):
        for kind in range(4):
            padded[channel, kind, :SUBS, :] = zeros
            padded[channel, 4 + kind, SUBS:, :] = zeros
    position_sums = [zeros, zeros]
    for channel in range(SUBS):
        strided = pl.ds(channel, devices, stride=SUBS)
        signal, gating, probing = (
            [fields[field, side, strided, :] for side in range(2)] for field in range(3)
        )
        windows_high, windows_low = [], []
        earlier = jnp.zeros((HALF, LANES), jnp.float32)
        for block in range(blocks):
            row = taps[pl.ds(block * SUBS + channel, 1), :]
            turned = pltpu.roll(
                jnp.broadcast_to(row, (HALF, LANES)), 0, axis=1, stride=1, stride_axis=0
            )
            high, low = halves(jnp.where(below, earlier, turned))
            windows_high.append(high)
            windows_low.append(low)
            earlier = turned
        turned = [half_turn(vals) for vals in signal]
        later = pltpu.roll(signal[1], 1, axis=0)
        later_turned = pltpu.roll(turned[1], 1, axis=0)
        later = jnp.where(row_ids == 0, 0.0, later)
        later_turned = jnp.where(row_ids == 0, 0.0, later_turned)
        kinds = (
            jnp.where(low_lanes, signal[0], later_turned),
            jnp.where(low_lanes, signal[1], turned[0]),
            jnp.where(low_lanes, turned[0], later),
            jnp.where(low_lanes, turned[1], signal[0]),
        )
        for kind in range(4):
            padded[channel, kind, SUBS:, :] = kinds[kind]
        left = jnp.concatenate(
            [
                jnp.concatenate(
                    [padded[channel, kind, SUBS - step : 2 * SUBS - step, :] for kind in range(4)],
                    axis=0,
                )
                for step in range(devices)
            ],
            axis=1,
        ).astype(jnp.bfloat16)
        right = jnp.concatenate(
            [
                jnp.concatenate([high, low], axis=1)
                for high, low in zip(windows_high, windows_low)
            ],
            axis=0,
        )
        parts = jnp.dot(left, right, preferred_element_type=jnp.float32)
        parts = parts[:, :LANES] + parts[:, LANES:]
        even, odd = (
            [parts[(2 * which + side) * SUBS : (2 * which + side + 1) * SUBS] for side in range(2)]
            for which in range(2)
        )
        odd_before = jnp.where(row_ids == 0, 0.0, pltpu.roll(odd[1], 1, axis=0))
        conv = (
            even[0] + half_turn(jnp.where(low_lanes, odd[0], odd_before)),
            even[1] + half_turn(jnp.where(low_lanes, odd[1], odd[0])),
        )
        back = []
        for side in range(2):
            mixed = gating[side] * conv[side]
            sigmoid_val = jax.nn.sigmoid(mixed)
            back.append(
                gating[side] * probing[side] * sigmoid_val * (1.0 + mixed * (1.0 - sigmoid_val))
            )
        next_row = jnp.where(row_ids == SUBS - 1, 0.0, pltpu.roll(back[0], SUBS - 1, axis=0))
        shifted = (
            half_turn(jnp.where(low_lanes, back[1], back[0])),
            half_turn(jnp.where(low_lanes, next_row, back[1])),
        )
        for kind, vals in enumerate((*back, *shifted)):
            padded[channel, 4 + kind, :SUBS, :] = vals

        def reach(kind, step):
            return padded[channel, 4 + kind, step : SUBS + step, :]

        pieces = []
        for block in range(blocks):
            step, odd_block = divmod(block, 2)
            if odd_block:
                group = (reach(1, step), reach(0, step + 1), reach(3, step), reach(2, step + 1))
            else:
                group = (reach(0, step), reach(1, step), reach(2, step), reach(3, step))
            pieces.append(jnp.concatenate(halves(jnp.concatenate(group, axis=0)), axis=0))
        left = jnp.concatenate(pieces, axis=1)
        right = jnp.concatenate(
            [jnp.concatenate(windows_high, axis=1), jnp.concatenate(windows_low, axis=1)], axis=0
        )
        parts = lax.dot_general(
            left, right, (((1,), (1,)), ((), ())), preferred_element_type=jnp.float32
        )
        parts = parts[: 4 * SUBS] + parts[4 * SUBS :]
        parts = parts + half_turn(parts)
        for side in range(2):
            grad = jnp.where(
                low_lanes,
                parts[side * SUBS : (side + 1) * SUBS],
                parts[(2 + side) * SUBS : (3 + side) * SUBS],
            )
            saliency = grad * signal[side]
            position_sums[side] += saliency
            place = (channel * 2 + side) * SUBS
            products[place : place + SUBS, :] = saliency
    pick = (iota((SUBS, LANES), 1) // BLOCK == iota((SUBS, LANES), 0)).astype(jnp.bfloat16)
    block_sums = sum(
        lax.dot_general(
            pick, term, (((1,), (1,)), ((), ())), preferred_element_type=jnp.float32
        )
        for term in halves(products[...])
    )
    for device in range(devices):
        rows = [vals[device : device + 1] for vals in position_sums] + [block_sums[:2]]
        message = jnp.concatenate(rows, axis=0)
        for copy in range(copies):
            sums_ref[device * copies + copy, :, :] = message


def weight_kernel(packed_ref, place_ref, weight_ref, scale_ref):
    devices = packed_ref.shape[0]
    members = devices * SUBS
    columns = weight_ref.shape[1]
    blocks_dev = 2 * LANES // BLOCK
    digits, offsets = [], []
    for source in range(devices):
        both = packed_ref[source, MEMBER_ROW:, :].astype(jnp.float32)
        digits.append(both[:SUBS])
        offsets.append(both[SUBS:] + float(source * blocks_dev))
    digits = jnp.concatenate(digits, axis=0)
    offsets = jnp.concatenate(offsets, axis=0)
    place = place_ref[...]
    place_rows = place.shape[0]
    row_pick = iota((members, place_rows), 1).astype(jnp.float32) == digits[:, :1]
    row_pick = row_pick.astype(jnp.bfloat16)
    lane_ids = iota((members, LANES), 1).astype(jnp.float32)
    low_digit = jnp.broadcast_to(digits[:, HALF : HALF + 1], (members, LANES))

    def looked_up(table):
        found = jnp.dot(
            row_pick, table.astype(jnp.float32).astype(jnp.bfloat16),
            preferred_element_type=jnp.float32,
        )
        return jnp.sum(jnp.where(lane_ids == low_digit, found, 0.0), axis=1, keepdims=True)

    targets = looked_up(place // LANES) * LANES + looked_up(place % LANES)
    targets = targets - (lax.axis_index("seq") * columns).astype(jnp.float32)
    node_pick = iota((members, columns), 1).astype(jnp.float32) == targets
    node_pick = node_pick.astype(jnp.float32)
    counts = jnp.sum(node_pick, axis=0, keepdims=True)
    scale_ref[...] = 1.0 / jnp.maximum(counts, 1.0)
    slot = iota((members, 2 * LANES), 1)
    inner = slot % LANES % (2 * SUBS)
    slot_block = (inner % SUBS) * 4 + (inner // SUBS) * 2 + slot // LANES
    own_block = jnp.broadcast_to(offsets[:, :1], (members, 2 * LANES))
    block_pick = (slot_block.astype(jnp.float32) == own_block).astype(jnp.float32)
    weight_ref[...] = lax.dot_general(
        block_pick.T.astype(jnp.bfloat16),
        node_pick.astype(jnp.bfloat16),
        (((1,), (0,)), ((), ())),
        preferred_element_type=jnp.float32,
    ).astype(jnp.bfloat16)


def finish_kernel(channel_count, sums_ref, weight_ref, scale_ref, position_ref, nodes_ref):
    copies = lax.axis_size("ch")
    devices = sums_ref.shape[0] // copies
    own = lax.axis_index("ch")
    total = sums_ref[0]
    for source in range(1, devices * copies):
        total = total + sums_ref[source]
    position_ref[...] = total[:2] / channel_count
    own_lanes = iota((SUBS, LANES), 1) // (2 * SUBS) == iota((SUBS, LANES), 0)
    rows = []
    for source in range(devices):
        message = sums_ref[source * copies + own]
        rows.append(
            jnp.concatenate(
                [jnp.where(own_lanes, message[2 + side : 3 + side], 0.0) for side in range(2)],
                axis=1,
            )
        )
    high, low = halves(jnp.concatenate(rows, axis=0))
    both = jnp.dot(
        jnp.concatenate([high, low], axis=0), weight_ref[...], preferred_element_type=jnp.float32
    )
    count = high.shape[0]
    nodes_ref[...] = (both[:count] + both[count:]) * scale_ref[...]


def whole_channels(
    inputs, gate_values, probe_values, filter_taps, member_blocks, member_nodes, node_place
):
    devices = lax.axis_size("seq")
    copies = lax.axis_size("ch")
    channels, length = inputs.shape
    columns = node_place.shape[0] // devices
    packed = pl.pallas_call(
        functools.partial(pack_kernel, length // BLOCK),
        out_shape=jax.ShapeDtypeStruct((devices, PACK_ROWS, LANES), jnp.bfloat16),
        name="pack",
    )(
        inputs,
        gate_values,
        probe_values,
        filter_taps,
        member_blocks.reshape(1, -1),
        member_nodes.reshape(1, -1),
    )
    packed = lax.all_to_all(packed, "seq", split_axis=0, concat_axis=0, tiled=True)
    sums = pl.pallas_call(
        saliency_kernel,
        out_shape=jax.ShapeDtypeStruct((devices * copies, 4, LANES), jnp.float32),
        scratch_shapes=[
            pltpu.VMEM((3, 2, devices * SUBS, LANES), jnp.float32),
            pltpu.VMEM((devices * FIELD_ROWS, LANES), jnp.float32),
            pltpu.VMEM((SUBS, 8, 2 * SUBS, LANES), jnp.float32),
            pltpu.VMEM((2 * SUBS * SUBS, LANES), jnp.float32),
        ],
        name="saliency",
    )(packed)
    sums = lax.all_to_all(sums, ("seq", "ch"), split_axis=0, concat_axis=0, tiled=True)
    weight, scale = pl.pallas_call(
        weight_kernel,
        out_shape=(
            jax.ShapeDtypeStruct((2 * LANES, columns), jnp.bfloat16),
            jax.ShapeDtypeStruct((1, columns), jnp.float32),
        ),
        name="weights",
    )(packed, node_place.reshape(-1, LANES))
    position, node_rows = pl.pallas_call(
        functools.partial(finish_kernel, channels * copies),
        out_shape=(
            jax.ShapeDtypeStruct((2, LANES), jnp.float32),
            jax.ShapeDtypeStruct((channels, columns), jnp.float32),
        ),
        name="finish",
    )(sums, weight, scale)
    return position.reshape(length), node_rows


def phase_table(rows_count, cols_count, modulus, sine_sign, row_start, col_start):
    row_ids = lax.broadcasted_iota(jnp.int32, (rows_count, cols_count), 0) + row_start
    col_ids = lax.broadcasted_iota(jnp.int32, (rows_count, cols_count), 1) + col_start
    angles = (row_ids * col_ids % modulus).astype(jnp.float32) * (2.0 * math.pi / modulus)
    return (jnp.cos(angles), sine_sign * jnp.sin(angles))


def complex_times(first_pair, second_pair):
    first_real, first_imag = first_pair
    second_real, second_imag = second_pair
    return (
        first_real * second_real - first_imag * second_imag,
        first_real * second_imag + first_imag * second_real,
    )


def complex_product(formula, first_pair, second_pair):
    first_real, first_imag = first_pair
    second_real, second_imag = second_pair
    real_part = jnp.einsum(formula, first_real, second_real, precision=HIGHEST) - jnp.einsum(
        formula, first_imag, second_imag, precision=HIGHEST
    )
    imag_part = jnp.einsum(formula, first_real, second_imag, precision=HIGHEST) + jnp.einsum(
        formula, first_imag, second_real, precision=HIGHEST
    )
    return (real_part, imag_part)


def split_sizes(length):
    return (length // 128, 128)


def local_forward(real_part, imag_part):
    stacks, rows_count, channels, length = real_part.shape
    outer_size, inner_size = split_sizes(length)
    data_pair = (
        real_part.reshape(-1, outer_size, inner_size),
        imag_part.reshape(-1, outer_size, inner_size),
    )
    part_pair = complex_product(
        "jn,rnm->rjm", phase_table(outer_size, outer_size, outer_size, -1.0, 0, 0), data_pair
    )
    part_pair = complex_times(part_pair, phase_table(outer_size, inner_size, length, -1.0, 0, 0))
    spec_real, spec_imag = complex_product(
        "rjn,nm->rjm", part_pair, phase_table(inner_size, inner_size, inner_size, -1.0, 0, 0)
    )
    new_shape = (stacks, rows_count * channels, outer_size, inner_size)
    return (spec_real.reshape(new_shape), spec_imag.reshape(new_shape))


def local_inverse(spec_real, spec_imag):
    stacks, rows_count, outer_size, inner_size = spec_real.shape
    length = outer_size * inner_size
    data_pair = (
        spec_real.reshape(-1, outer_size, inner_size),
        spec_imag.reshape(-1, outer_size, inner_size),
    )
    part_pair = complex_product(
        "rjn,nm->rjm", data_pair, phase_table(inner_size, inner_size, inner_size, 1.0, 0, 0)
    )
    part_pair = complex_times(part_pair, phase_table(outer_size, inner_size, length, 1.0, 0, 0))
    out_real, out_imag = complex_product(
        "jn,rnm->rjm", phase_table(outer_size, outer_size, outer_size, 1.0, 0, 0), part_pair
    )
    return (
        out_real.reshape(stacks, rows_count, length),
        out_imag.reshape(stacks, rows_count, length),
    )


def spectrum_full(columns, seq_index, send):
    stacks, devices, channels, col_width = columns.shape
    modulus = 2 * devices * devices * col_width
    flattened = columns.reshape(stacks, devices, channels * col_width)
    row_cos, row_sin = phase_table(2 * devices, devices, 2 * devices, -1.0, 0, 0)
    grid_shape = (stacks, 2 * devices, channels, col_width)
    real_part = jnp.einsum("kn,snm->skm", row_cos, flattened, precision=HIGHEST).reshape(grid_shape)
    imag_part = jnp.einsum("kn,snm->skm", row_sin, flattened, precision=HIGHEST).reshape(grid_shape)
    turn_cos, turn_sin = phase_table(
        2 * devices, col_width, modulus, -1.0, 0, seq_index * col_width
    )
    real_part, imag_part = complex_times(
        (real_part, imag_part), (turn_cos[:, None, :], turn_sin[:, None, :])
    )
    real_part, imag_part = send(real_part, imag_part)
    return local_forward(real_part, imag_part)


def signal_full(spec_real, spec_imag, seq_index, devices, send):
    real_part, imag_part = local_inverse(spec_real, spec_imag)
    stacks, rows_count, length = real_part.shape
    channels = rows_count // 2
    modulus = 2 * devices * length
    real_part = real_part.reshape(stacks, 2, channels, length)
    imag_part = imag_part.reshape(stacks, 2, channels, length)
    turn_cos, turn_sin = phase_table(2, length, modulus, 1.0, 2 * seq_index, 0)
    real_part, imag_part = complex_times(
        (real_part, imag_part), (turn_cos[:, None, :], turn_sin[:, None, :])
    )
    real_part, imag_part = send(real_part, imag_part)
    col_width = length // devices
    back_cos, back_sin = phase_table(devices, 2 * devices, 2 * devices, 1.0, 0, 0)
    flat_real = real_part.reshape(stacks, 2 * devices, channels * col_width)
    flat_imag = imag_part.reshape(stacks, 2 * devices, channels * col_width)
    signal_vals = (
        jnp.einsum("ak,skm->sam", back_cos, flat_real, precision=HIGHEST)
        - jnp.einsum("ak,skm->sam", back_sin, flat_imag, precision=HIGHEST)
    ) / modulus
    return signal_vals.reshape(stacks, devices, channels, col_width)


def cotangent(conv_vals, gating, probing):
    gate_wide = gating.astype(jnp.float32)
    mixed = gate_wide * conv_vals
    sigmoid_val = jax.nn.sigmoid(mixed)
    return (
        gate_wide * probing.astype(jnp.float32) * sigmoid_val * (1.0 + mixed * (1.0 - sigmoid_val))
    )


def spread_channels(
    inputs, gate_values, probe_values, filter_taps, member_blocks, member_nodes, node_place
):
    seq_index = lax.axis_index("seq")
    devices = lax.axis_size("seq")
    channels, length = inputs.shape
    inputs_wide = inputs.astype(jnp.float32)
    stacked = jnp.stack([inputs_wide, filter_taps]).reshape(2, 1, channels, length)
    columns_pair = lax.all_to_all(stacked, "seq", split_axis=3, concat_axis=1, tiled=True)

    def send_input(real_part, imag_part):
        return (
            lax.all_to_all(real_part, "seq", split_axis=1, concat_axis=3, tiled=True),
            lax.all_to_all(imag_part, "seq", split_axis=1, concat_axis=3, tiled=True),
        )

    def send_output(real_part, imag_part):
        return (
            lax.all_to_all(real_part, "seq", split_axis=3, concat_axis=1, tiled=True),
            lax.all_to_all(imag_part, "seq", split_axis=3, concat_axis=1, tiled=True),
        )

    def send_cotangent(real_part, imag_part):
        return (
            lax.all_to_all(real_part, "seq", split_axis=1, concat_axis=3, tiled=True),
            lax.all_to_all(imag_part, "seq", split_axis=1, concat_axis=3, tiled=True),
        )

    def send_gradient(real_part, imag_part):
        return (
            lax.all_to_all(real_part, "seq", split_axis=3, concat_axis=1, tiled=True),
            lax.all_to_all(imag_part, "seq", split_axis=3, concat_axis=1, tiled=True),
        )

    forward_section, inverse_section = (spectrum_full, signal_full)
    spec_real, spec_imag = forward_section(columns_pair, seq_index, send_input)
    filter_pair = (spec_real[1], spec_imag[1])
    conv_real, conv_imag = complex_times((spec_real[0], spec_imag[0]), filter_pair)
    conv_cols = inverse_section(conv_real[None], conv_imag[None], seq_index, devices, send_output)
    conv_rows = lax.all_to_all(conv_cols, "seq", split_axis=1, concat_axis=3, tiled=True).reshape(
        channels, length
    )
    back_rows = cotangent(conv_rows, gate_values, probe_values)
    back_cols = lax.all_to_all(
        back_rows.reshape(1, 1, channels, length), "seq", split_axis=3, concat_axis=1, tiled=True
    )
    back_real, back_imag = forward_section(back_cols, seq_index, send_cotangent)
    grad_real = back_real[0] * filter_pair[0] + back_imag[0] * filter_pair[1]
    grad_imag = back_imag[0] * filter_pair[0] - back_real[0] * filter_pair[1]
    grad_cols = inverse_section(grad_real[None], grad_imag[None], seq_index, devices, send_gradient)
    returned = lax.all_to_all(grad_cols, "seq", split_axis=1, concat_axis=3, tiled=True).reshape(
        channels, length
    )
    saliency = returned * inputs_wide
    channel_count = channels * lax.axis_size("ch")
    position_saliency = lax.psum(jnp.sum(saliency, axis=0), "ch") / channel_count
    blocks_dev = length // BLOCK
    block_rows = jnp.sum(saliency.reshape(channels, blocks_dev, BLOCK), axis=2)
    local_blocks = member_blocks - seq_index * blocks_dev
    targets = node_place[member_nodes]
    member_rows = jnp.take(block_rows, local_blocks, axis=1)
    nodes_dev = NODES // devices
    gathered_rows, gathered_targets = (
        lax.all_gather(member_rows, "seq", axis=1, tiled=True),
        lax.all_gather(targets.astype(jnp.float32), "seq", axis=0, tiled=True),
    )
    owned_ids = gathered_targets.astype(jnp.int32) - seq_index * nodes_dev
    slot_ids = jnp.where((owned_ids >= 0) & (owned_ids < nodes_dev), owned_ids, nodes_dev)
    node_sums = jax.ops.segment_sum(gathered_rows.T, slot_ids, num_segments=nodes_dev + 1)[
        :nodes_dev
    ].T
    node_counts = jax.ops.segment_sum(
        jnp.ones(slot_ids.shape, jnp.float32), slot_ids, num_segments=nodes_dev + 1
    )[:nodes_dev]
    node_rows = node_sums / jnp.maximum(node_counts, 1.0)[None, :]
    return (position_saliency, node_rows)


def per_device(*args):
    channels, length = args[0].shape
    devices = lax.axis_size("seq")
    members = args[4].shape[0]
    fits = channels == SUBS * devices and devices == SUBS and length == 2 * LANES
    if fits and members == SUBS and NODES % (devices * LANES) == 0:
        return whole_channels(*args)
    return spread_channels(*args)


def solution(mesh):
    placed = (
        P("ch", "seq"),
        P("ch", "seq"),
        P("ch", "seq"),
        P("ch", "seq"),
        P("seq"),
        P("seq"),
        P(),
    )
    return jax.shard_map(
        per_device,
        mesh=mesh,
        in_specs=placed,
        out_specs=(P("seq"), P("ch", "seq")),
        check_vma=False,
    )
```

profile of v0, /device:TPU:0, one launch (start us, length us, event | category | flops | bytes accessed | tf_op | source)
XLA Modules:
  0.0 35.9 jit_solution(3668180693544072894)
XLA Ops:
  0.6 1.6 %pack.1 = bf16[8,96,128]{2,1,0:T(8,128)(2,1)} custom-call(bf16[64,256]{1,0:T(8,128)(2,1)} %inputs_ref.1, bf16[64,256]{1,0:T(8,128)(2,1)} %gate_ref.1, bf16[64,256]{1,0:T(8,128)(2,1)} %probe_ref.1, f32[64,256]{1,0:T(8,128)} %taps_ref.1, s32[1,8]{1,0:T(1,128)} %bitcast.5, s32[1,8]{1,0:T(1,128)} %bitcast.6), custom_call_target="tpu_custom_call" | custom-call | tf_op jit(solution)/shard_map/pack/pallas_call | solution.py:294
  2.3 15.3 %all_to_all.10.packed_ref = bf16[8,96,128]{2,1,0:T(8,128)(2,1)} all-to-all(bf16[8,96,128]{2,1,0:T(8,128)(2,1)} %pack.1), channel_id=1, replica_groups=mesh['seq'=8,'ch'=4] {'seq'}, dimensions={0} | all-to-all | bytes 393216 | tf_op jit(solution)/shard_map/all_to_all | solution.py:306
  17.6 5.1 %saliency.1 = f32[32,4,128]{2,1,0:T(4,128)} custom-call(bf16[8,96,128]{2,1,0:T(8,128)(2,1)} %all_to_all.10.packed_ref), custom_call_target="tpu_custom_call" | custom-call | tf_op jit(solution)/shard_map/saliency/pallas_call | solution.py:307
  22.7 3.2 %all-to-all-start.1 = ((f32[32,4,128]{2,1,0:T(4,128)}), f32[32,4,128]{2,1,0:T(4,128)S(1)}, u32[]{:S(2)}, u32[]{:S(2)}) async-start(f32[32,4,128]{2,1,0:T(4,128)} %saliency.1), calls=%async_computation.1 | async-start | bytes 131072 | tf_op jit(solution)/shard_map/all_to_all | solution.py:318
  25.8 2.3 %weights.1 = (bf16[256,1024]{1,0:T(8,128)(2,1)}, f32[1,1024]{1,0:T(1,128)}) custom-call(bf16[8,96,128]{2,1,0:T(8,128)(2,1)} %all_to_all.10.packed_ref, s32[64,128]{1,0:T(8,128)} %bitcast.4), custom_call_target="tpu_custom_call" | custom-call | tf_op jit(solution)/shard_map/weights/pallas_call | solution.py:319
  28.1 5.1 %all-to-all-done.1.sums_ref = f32[32,4,128]{2,1,0:T(4,128)S(1)} async-done(((f32[32,4,128]{2,1,0:T(4,128)}), f32[32,4,128]{2,1,0:T(4,128)S(1)}, u32[]{:S(2)}, u32[]{:S(2)}) %all-to-all-start.1) | async-done | bytes 65568 | tf_op jit(solution)/shard_map/all_to_all | solution.py:318
  33.2 0.0 copy-start
  33.2 0.6 %copy-done = f32[32,4,128]{2,1,0:T(4,128)} copy-done((f32[32,4,128]{2,1,0:T(4,128)}, f32[32,4,128]{2,1,0:T(4,128)S(1)}, u32[]{:S(2)}) %copy-start) | copy-done | bytes 65560
  33.9 2.0 %finish.1 = (f32[2,128]{1,0:T(2,128)}, f32[64,1024]{1,0:T(8,128)}) custom-call(f32[32,4,128]{2,1,0:T(4,128)} %copy-done, bf16[256,1024]{1,0:T(8,128)(2,1)} %get-tuple-element.6.weight_ref, f32[1,1024]{1,0:T(1,128)} %get-tuple-element.7.scale_ref), custom_call_target="tpu_custom_call" | custom-call | tf_op jit(solution)/shard_map/finish/pallas_call | solution.py:327
Async XLA Ops:
  22.7 10.6 %all-to-all-start.1 = ((f32[32,4,128]{2,1,0:T(4,128)}), f32[32,4,128]{2,1,0:T(4,128)S(1)}, u32[]{:S(2)}, u32[]{:S(2)}) async-start(f32[32,4,128]{2,1,0:T(4,128)} %saliency.1), calls=%async_computation.1 | async-start | bytes 131072 | tf_op jit(solution)/shard_map/all_to_all | solution.py:318
  33.2 0.6 %copy-start = (f32[32,4,128]{2,1,0:T(4,128)}, f32[32,4,128]{2,1,0:T(4,128)S(1)}, u32[]{:S(2)}) copy-start(f32[32,4,128]{2,1,0:T(4,128)S(1)} %all-to-all-done.1.sums_ref) | copy-start | bytes 196612
where the time goes:
time: 36.2 us; the launch traced here: 35.9 us
  blocking collectives  15.3 us (42%)
  Pallas kernels  11 us (30%)
  waiting for transfers between devices  5.11 us (14%)
  starting transfers between devices  3.16 us (9%)
  between operations  0.64 us (2%)
  local copies, waits for them, and re-layouts  0.63 us (2%)
    all_to_all x1, blocking collectives, whole_channels(): lax.all_to_all(packed, 'seq', split_axis=0, concat_axis=0, tiled=True)  15.3 us
    all_to_all x1, waiting for transfers between devices, whole_channels(): lax.all_to_all(sums, ('seq', 'ch'), split_axis=0, concat_axis=0, tiled=True)  5.11 us
    pallas_call x1, Pallas kernels, whole_channels(): pl.pallas_call(saliency_kernel, out_shape=jax.ShapeDtypeStruct((devices *...  5.06 us
    all_to_all x1, starting transfers between devices, whole_channels(): lax.all_to_all(sums, ('seq', 'ch'), split_axis=0, concat_axis=0, tiled=True)  3.16 us
    pallas_call x1, Pallas kernels, whole_channels(): pl.pallas_call(weight_kernel, out_shape=(jax.ShapeDtypeStruct((2 * LANES,...  2.3 us
    pallas_call x1, Pallas kernels, whole_channels(): pl.pallas_call(functools.partial(finish_kernel, channels * copies), out_s...  1.98 us
    pallas_call x1, Pallas kernels, whole_channels(): pl.pallas_call(functools.partial(pack_kernel, length // BLOCK), out_shape...  1.63 us
  transfers between devices with their start and end apart: 1, of which 1 were waited for; matrix products, arithmetic and copies ran while one was open for 0% of the time, Pallas kernels for 6%

commit v1 on v0

--- a/solution.py
+++ b/solution.py
@@ -20,6 +20,7 @@
 
 
 HIGHEST = lax.Precision.HIGHEST
+LEAN = pltpu.CompilerParams(vmem_limit_bytes=16 * 1024 * 1024)
 
 
 def iota(shape, dim):
@@ -31,10 +32,18 @@
     return high, (vals - high.astype(jnp.float32)).astype(jnp.bfloat16)
 
 
-def pack_kernel(
-    blocks_dev, inputs_ref, gate_ref, probe_ref, taps_ref, blocks_ref, nodes_ref, packed_ref
-):
+def pack_kernel(blocks_dev, *refs):
+    sources, packed_ref, arrived, landed = refs[:6], refs[6], refs[7:13], refs[13]
+    inputs_ref, gate_ref, probe_ref, taps_ref, blocks_ref, nodes_ref = arrived
     devices = packed_ref.shape[0]
+    loads = [
+        pltpu.make_async_copy(source, target, landed.at[place])
+        for place, (source, target) in enumerate(zip(sources, arrived))
+    ]
+    for load in loads:
+        load.start()
+    for load in loads:
+        load.wait()
 
     def put(pair, field, tiles):
         for side in range(2):
@@ -70,13 +79,61 @@
     return pltpu.roll(vals, HALF, axis=1)
 
 
-def saliency_kernel(packed_ref, sums_ref, fields, taps, padded, products):
+def fill_weights(packed_ref, place_ref, weight_ref, scale_ref):
+    devices = packed_ref.shape[0]
+    members = devices * SUBS
+    columns = weight_ref.shape[1]
+    blocks_dev = 2 * LANES // BLOCK
+    digits, offsets = [], []
+    for source in range(devices):
+        both = packed_ref[source, MEMBER_ROW:, :].astype(jnp.float32)
+        digits.append(both[:SUBS])
+        offsets.append(both[SUBS:] + float(source * blocks_dev))
+    digits = jnp.concatenate(digits, axis=0)
+    offsets = jnp.concatenate(offsets, axis=0)
+    place = place_ref[...]
+    place_rows = place.shape[0]
+    row_pick = iota((members, place_rows), 1).astype(jnp.float32) == digits[:, :1]
+    row_pick = row_pick.astype(jnp.bfloat16)
+    lane_ids = iota((members, LANES), 1).astype(jnp.float32)
+    low_digit = jnp.broadcast_to(digits[:, HALF : HALF + 1], (members, LANES))
+
+    def looked_up(table):
+        found = jnp.dot(
+            row_pick, table.astype(jnp.float32).astype(jnp.bfloat16),
+            preferred_element_type=jnp.float32,
+        )
+        return jnp.sum(jnp.where(lane_ids == low_digit, found, 0.0), axis=1, keepdims=True)
+
+    targets = looked_up(place // LANES) * LANES + looked_up(place % LANES)
+    targets = targets - (lax.axis_index("seq") * columns).astype(jnp.float32)
+    node_pick = iota((members, columns), 1).astype(jnp.float32) == targets
+    node_pick = node_pick.astype(jnp.float32)
+    counts = jnp.sum(node_pick, axis=0, keepdims=True)
+    scale_ref[...] = 1.0 / jnp.maximum(counts, 1.0)
+    slot = iota((members, 2 * LANES), 1)
+    inner = slot % LANES % (2 * SUBS)
+    slot_block = (inner % SUBS) * 4 + (inner // SUBS) * 2 + slot // LANES
+    own_block = jnp.broadcast_to(offsets[:, :1], (members, 2 * LANES))
+    block_pick = (slot_block.astype(jnp.float32) == own_block).astype(jnp.float32)
+    weight_ref[...] = lax.dot_general(
+        block_pick.T.astype(jnp.bfloat16),
+        node_pick.astype(jnp.bfloat16),
+        (((1,), (0,)), ((), ())),
+        preferred_element_type=jnp.float32,
+    ).astype(jnp.bfloat16)
+
+
+def saliency_kernel(
+    packed_ref, place_ref, sums_ref, weight_ref, scale_ref, fields, taps, padded, products
+):
     devices = packed_ref.shape[0]
     blocks = 2 * devices
     copies = sums_ref.shape[0] // devices
     low_lanes = iota((SUBS, LANES), 1) < HALF
     row_ids = iota((SUBS, LANES), 0)
     below = iota((HALF, LANES), 1) < iota((HALF, LANES), 0)
+    fill_weights(packed_ref, place_ref, weight_ref, scale_ref)
     for source in range(devices):
         rows = slice(source * SUBS, (source + 1) * SUBS)
         for field in range(3):
@@ -213,51 +270,6 @@
             sums_ref[device * copies + copy, :, :] = message
 
 
-def weight_kernel(packed_ref, place_ref, weight_ref, scale_ref):
-    devices = packed_ref.shape[0]
-    members = devices * SUBS
-    columns = weight_ref.shape[1]
-    blocks_dev = 2 * LANES // BLOCK
-    digits, offsets = [], []
-    for source in range(devices):
-        both = packed_ref[source, MEMBER_ROW:, :].astype(jnp.float32)
-        digits.append(both[:SUBS])
-        offsets.append(both[SUBS:] + float(source * blocks_dev))
-    digits = jnp.concatenate(digits, axis=0)
-    offsets = jnp.concatenate(offsets, axis=0)
-    place = place_ref[...]
-    place_rows = place.shape[0]
-    row_pick = iota((members, place_rows), 1).astype(jnp.float32) == digits[:, :1]
-    row_pick = row_pick.astype(jnp.bfloat16)
-    lane_ids = iota((members, LANES), 1).astype(jnp.float32)
-    low_digit = jnp.broadcast_to(digits[:, HALF : HALF + 1], (members, LANES))
-
-    def looked_up(table):
-        found = jnp.dot(
-            row_pick, table.astype(jnp.float32).astype(jnp.bfloat16),
-            preferred_element_type=jnp.float32,
-        )
-        return jnp.sum(jnp.where(lane_ids == low_digit, found, 0.0), axis=1, keepdims=True)
-
-    targets = looked_up(place // LANES) * LANES + looked_up(place % LANES)
-    targets = targets - (lax.axis_index("seq") * columns).astype(jnp.float32)
-    node_pick = iota((members, columns), 1).astype(jnp.float32) == targets
-    node_pick = node_pick.astype(jnp.float32)
-    counts = jnp.sum(node_pick, axis=0, keepdims=True)
-    scale_ref[...] = 1.0 / jnp.maximum(counts, 1.0)
-    slot = iota((members, 2 * LANES), 1)
-    inner = slot % LANES % (2 * SUBS)
-    slot_block = (inner % SUBS) * 4 + (inner // SUBS) * 2 + slot // LANES
-    own_block = jnp.broadcast_to(offsets[:, :1], (members, 2 * LANES))
-    block_pick = (slot_block.astype(jnp.float32) == own_block).astype(jnp.float32)
-    weight_ref[...] = lax.dot_general(
-        block_pick.T.astype(jnp.bfloat16),
-        node_pick.astype(jnp.bfloat16),
-        (((1,), (0,)), ((), ())),
-        preferred_element_type=jnp.float32,
-    ).astype(jnp.bfloat16)
-
-
 def finish_kernel(channel_count, sums_ref, weight_ref, scale_ref, position_ref, nodes_ref):
     copies = lax.axis_size("ch")
     devices = sums_ref.shape[0] // copies
@@ -291,11 +303,7 @@
     copies = lax.axis_size("ch")
     channels, length = inputs.shape
     columns = node_place.shape[0] // devices
-    packed = pl.pallas_call(
-        functools.partial(pack_kernel, length // BLOCK),
-        out_shape=jax.ShapeDtypeStruct((devices, PACK_ROWS, LANES), jnp.bfloat16),
-        name="pack",
-    )(
+    local = (
         inputs,
         gate_values,
         probe_values,
@@ -303,33 +311,40 @@
         member_blocks.reshape(1, -1),
         member_nodes.reshape(1, -1),
     )
+    packed = pl.pallas_call(
+        functools.partial(pack_kernel, length // BLOCK),
+        out_shape=jax.ShapeDtypeStruct((devices, PACK_ROWS, LANES), jnp.bfloat16),
+        in_specs=[pl.BlockSpec(memory_space=pltpu.HBM)] * len(local),
+        scratch_shapes=[pltpu.VMEM(part.shape, part.dtype) for part in local]
+        + [pltpu.SemaphoreType.DMA((len(local),))],
+        compiler_params=LEAN,
+        name="pack",
+    )(*(pltpu.with_memory_space_constraint(part, pltpu.HBM) for part in local))
     packed = lax.all_to_all(packed, "seq", split_axis=0, concat_axis=0, tiled=True)
-    sums = pl.pallas_call(
+    sums, weight, scale = pl.pallas_call(
         saliency_kernel,
-        out_shape=jax.ShapeDtypeStruct((devices * copies, 4, LANES), jnp.float32),
+        out_shape=(
+            jax.ShapeDtypeStruct((devices * copies, 4, LANES), jnp.float32),
+            jax.ShapeDtypeStruct((2 * LANES, columns), jnp.bfloat16),
+            jax.ShapeDtypeStruct((1, columns), jnp.float32),
+        ),
         scratch_shapes=[
             pltpu.VMEM((3, 2, devices * SUBS, LANES), jnp.float32),
             pltpu.VMEM((devices * FIELD_ROWS, LANES), jnp.float32),
             pltpu.VMEM((SUBS, 8, 2 * SUBS, LANES), jnp.float32),
             pltpu.VMEM((2 * SUBS * SUBS, LANES), jnp.float32),
         ],
+        compiler_params=LEAN,
         name="saliency",
-    )(packed)
+    )(packed, node_place.reshape(-1, LANES))
     sums = lax.all_to_all(sums, ("seq", "ch"), split_axis=0, concat_axis=0, tiled=True)
-    weight, scale = pl.pallas_call(
-        weight_kernel,
-        out_shape=(
-            jax.ShapeDtypeStruct((2 * LANES, columns), jnp.bfloat16),
-            jax.ShapeDtypeStruct((1, columns), jnp.float32),
-        ),
-        name="weights",
-    )(packed, node_place.reshape(-1, LANES))
     position, node_rows = pl.pallas_call(
         functools.partial(finish_kernel, channels * copies),
         out_shape=(
             jax.ShapeDtypeStruct((2, LANES), jnp.float32),
             jax.ShapeDtypeStruct((channels, columns), jnp.float32),
         ),
+        compiler_params=LEAN,
         name="finish",
     )(sums, weight, scale)
     return position.reshape(length), node_rows

time: 36.2 us -> 31.9 us (0.88)
  blocking collectives: 15.3 us -> 25.4 us
  Pallas kernels: 11 us -> 5.56 us
  waiting for transfers between devices: 5.11 us -> 0 us
  starting transfers between devices: 3.16 us -> 0 us
  local copies, waits for them, and re-layouts: 0.63 us -> 0.01 us
    all_to_all x0 -> x1, blocking collectives: none -> 10.4 us  [whole_channels(): lax.all_to_all(sums, ('seq', 'ch'), split_axis=0, concat_axis=0, tiled=True)]
    all_to_all x1 -> x0, waiting for transfers between devices: 5.11 us -> none  [whole_channels(): lax.all_to_all(sums, ('seq', 'ch'), split_axis=0, concat_axis=0, tiled=True)]
    pallas_call x2 -> x1, Pallas kernels: 7.36 us -> 3.56 us  [whole_channels(): pl.pallas_call(saliency_kernel, out_shape=(jax.ShapeDtypeStruct((devices...]
    all_to_all x1 -> x0, starting transfers between devices: 3.16 us -> none  [whole_channels(): lax.all_to_all(sums, ('seq', 'ch'), split_axis=0, concat_axis=0, tiled=True)]
    pallas_call x1, Pallas kernels: 1.98 us -> 0.94 us  [whole_channels(): pl.pallas_call(functools.partial(finish_kernel, channels * copies), out_s...]
    unnamed x2, local copies, waits for them, and re-layouts: 0.63 us -> 0.01 us
    pallas_call x1, Pallas kernels: 1.63 us -> 1.07 us  [whole_channels(): pl.pallas_call(functools.partial(pack_kernel, length // BLOCK), out_shape...]
  transfers between devices with their start and end apart: 1 -> 0, of which waited for: 1 -> 0; matrix products, arithmetic and copies ran while one was open for 0% -> 0% of each run, Pallas kernels for 6% -> 0%
where the time goes in v1:
time: 31.9 us; the launch traced here: 31.6 us
  blocking collectives  25.4 us (80%)
  Pallas kernels  5.56 us (17%)
  between operations  0.66 us (2%)
    all_to_all x1, blocking collectives, whole_channels(): lax.all_to_all(packed, 'seq', split_axis=0, concat_axis=0, tiled=True)  15 us
    all_to_all x1, blocking collectives, whole_channels(): lax.all_to_all(sums, ('seq', 'ch'), split_axis=0, concat_axis=0, tiled=True)  10.4 us
    pallas_call x1, Pallas kernels, whole_channels(): pl.pallas_call(saliency_kernel, out_shape=(jax.ShapeDtypeStruct((devices...  3.56 us
    pallas_call x1, Pallas kernels, whole_channels(): pl.pallas_call(functools.partial(pack_kernel, length // BLOCK), out_shape...  1.07 us
    pallas_call x1, Pallas kernels, whole_channels(): pl.pallas_call(functools.partial(finish_kernel, channels * copies), out_s...  0.94 us

profile of v1, /device:TPU:0, one launch (start us, length us, event | category | flops | bytes accessed | tf_op | source)
XLA Modules:
  0.0 31.6 jit_solution(13811407181903749644)
XLA Ops:
  0.6 1.1 %pack.1 = bf16[8,96,128]{2,1,0:T(8,128)(2,1)S(1)} custom-call(bf16[64,256]{1,0:T(8,128)(2,1)} %refs_0_.1, bf16[64,256]{1,0:T(8,128)(2,1)} %refs_1_.1, bf16[64,256]{1,0:T(8,128)(2,1)} %refs_2_.1, f32[64,256]{1,0:T(8,128)} %refs_3_.1, s32[1,8]{1,0:T(1,128)} %bitcast.5, s32[1,8]{1,0:T(1,128)} %bitcast.6), custom_call_target="tpu_custom_call" | custom-call | tf_op jit(solution)/shard_map/pack/pallas_call | solution.py:314
  1.7 0.0 copy-start
  1.7 15.0 %all_to_all.10.packed_ref = bf16[8,96,128]{2,1,0:T(8,128)(2,1)S(1)} all-to-all(bf16[8,96,128]{2,1,0:T(8,128)(2,1)S(1)} %pack.1), channel_id=1, replica_groups=mesh['seq'=8,'ch'=4] {'seq'}, dimensions={0} | all-to-all | bytes 393216 | tf_op jit(solution)/shard_map/all_to_all | solution.py:323
  16.7 0.0 copy-done
  16.8 3.6 %saliency.1 = (f32[32,4,128]{2,1,0:T(4,128)S(1)}, bf16[256,1024]{1,0:T(8,128)(2,1)S(1)}, f32[1,1024]{1,0:T(1,128)S(1)}) custom-call(bf16[8,96,128]{2,1,0:T(8,128)(2,1)S(1)} %all_to_all.10.packed_ref, s32[64,128]{1,0:T(8,128)S(1)} %bitcast.4), custom_call_target="tpu_custom_call" | custom-call | tf_op jit(solution)/shard_map/saliency/pallas_call | solution.py:324
  20.3 10.4 %all_to_all.11.sums_ref = f32[32,4,128]{2,1,0:T(4,128)S(1)} all-to-all(f32[32,4,128]{2,1,0:T(4,128)S(1)} %get-tuple-element.7), channel_id=1, replica_groups=mesh['seq'=8,'ch'=4] {'seq','ch'}, dimensions={0} | all-to-all | bytes 131072 | tf_op jit(solution)/shard_map/all_to_all | solution.py:340
  30.7 0.9 %finish.1 = (f32[2,128]{1,0:T(2,128)}, f32[64,1024]{1,0:T(8,128)}) custom-call(f32[32,4,128]{2,1,0:T(4,128)S(1)} %all_to_all.11.sums_ref, bf16[256,1024]{1,0:T(8,128)(2,1)S(1)} %get-tuple-element.8.weight_ref, f32[1,1024]{1,0:T(1,128)S(1)} %get-tuple-element.9.scale_ref), custom_call_target="tpu_custom_call" | custom-call | tf_op jit(solution)/shard_map/finish/pallas_call | solution.py:341
Async XLA Ops:
  1.7 15.0 %copy-start = (s32[8192]{0:T(1024)S(1)}, s32[8192]{0:T(1024)}, u32[]{:S(2)}) copy-start(s32[8192]{0:T(1024)} %param.13) | copy-start | bytes 98308

commit v2 on v1

--- a/solution.py
+++ b/solution.py
@@ -13,6 +13,8 @@
 LANES = 128
 SUBS = 8
 HALF = LANES // 2
+PART = 32
+PARTS = LANES // PART
 FIELD_ROWS = 16
 FIELDS = 5
 MEMBER_ROW = FIELDS * FIELD_ROWS
@@ -73,10 +75,6 @@
     member_rows = jnp.concatenate([digits, places], axis=0).astype(jnp.bfloat16)
     for device in range(devices):
         packed_ref[device, MEMBER_ROW:, :] = member_rows
-
-
-def half_turn(vals):
-    return pltpu.roll(vals, HALF, axis=1)
 
 
 def fill_weights(packed_ref, place_ref, weight_ref, scale_ref):
@@ -112,8 +110,7 @@
     counts = jnp.sum(node_pick, axis=0, keepdims=True)
     scale_ref[...] = 1.0 / jnp.maximum(counts, 1.0)
     slot = iota((members, 2 * LANES), 1)
-    inner = slot % LANES % (2 * SUBS)
-    slot_block = (inner % SUBS) * 4 + (inner // SUBS) * 2 + slot // LANES
+    slot_block = slot % (2 * SUBS) * 2 + slot // LANES
     own_block = jnp.broadcast_to(offsets[:, :1], (members, 2 * LANES))
     block_pick = (slot_block.astype(jnp.float32) == own_block).astype(jnp.float32)
     weight_ref[...] = lax.dot_general(
@@ -124,139 +121,133 @@
     ).astype(jnp.bfloat16)
 
 
+def windows(taps, channel, first_turn, from_earlier):
+    rows = []
+    earlier = jnp.zeros((PART, LANES), jnp.float32)
+    for block in range(taps.shape[0] // SUBS):
+        row = jnp.broadcast_to(taps[pl.ds(block * SUBS + channel, 1), :], (PART, LANES))
+        turned = pltpu.roll(row, first_turn, axis=1, stride=1, stride_axis=0)
+        rows.append(jnp.concatenate(halves(jnp.where(from_earlier, earlier, turned)), axis=1))
+        earlier = turned
+    return jnp.concatenate(rows, axis=0)
+
+
+def by_part(pieces):
+    blocks = pieces[0].shape[0]
+    lanes = iota((blocks, LANES), 1)
+    result = pieces[-1]
+    for part in range(len(pieces) - 2, -1, -1):
+        result = jnp.where(lanes < (part + 1) * PART, pieces[part], result)
+    return result
+
+
+def turn(vals, parts):
+    shift = parts * PART % LANES
+    return pltpu.roll(vals, shift, axis=1) if shift else vals
+
+
+def spread(rows, padded, single, sign):
+    blocks = rows.shape[0]
+    start = blocks if sign < 0 else 0
+    zeros = jnp.zeros((blocks, LANES), jnp.float32)
+    single[start : start + blocks, :] = rows
+    single[blocks - start : 2 * blocks - start, :] = zeros
+    moved = [single[start + sign * step : start + sign * step + blocks, :] for step in range(PARTS)]
+    for part in range(PARTS):
+        joined = by_part([turn(moved[step], step - part) for step in range(PARTS)])
+        padded[part, start : start + blocks, :] = joined
+        padded[part, blocks - start : 2 * blocks - start, :] = zeros
+    columns = []
+    for step in range(0, blocks, PARTS):
+        offset = start + sign * step
+        columns.append(
+            jnp.concatenate(
+                [padded[part, offset : offset + blocks, :] for part in range(PARTS)], axis=0
+            )
+        )
+    return jnp.concatenate(columns, axis=1)
+
+
+def next_block(vals, sign):
+    blocks = vals.shape[0]
+    row_ids = iota((blocks, LANES), 0)
+    if sign < 0:
+        return jnp.where(row_ids == 0, 0.0, pltpu.roll(vals, 1, axis=0))
+    return jnp.where(row_ids == blocks - 1, 0.0, pltpu.roll(vals, blocks - 1, axis=0))
+
+
 def saliency_kernel(
-    packed_ref, place_ref, sums_ref, weight_ref, scale_ref, fields, taps, padded, products
+    packed_ref,
+    place_ref,
+    sums_ref,
+    weight_ref,
+    scale_ref,
+    fields,
+    taps,
+    taps_turned,
+    single,
+    padded,
+    products,
 ):
     devices = packed_ref.shape[0]
     blocks = 2 * devices
     copies = sums_ref.shape[0] // devices
-    low_lanes = iota((SUBS, LANES), 1) < HALF
-    row_ids = iota((SUBS, LANES), 0)
-    below = iota((HALF, LANES), 1) < iota((HALF, LANES), 0)
-    fill_weights(packed_ref, place_ref, weight_ref, scale_ref)
+    row_ids, lane_ids = iota((PART, LANES), 0), iota((PART, LANES), 1)
+    lanes = iota((blocks, LANES), 1)
+    terms = []
+    for term in range(2):
+        place = slice((3 + term) * FIELD_ROWS, (4 + term) * FIELD_ROWS)
+        terms.append(
+            jnp.concatenate([packed_ref[source, place, :] for source in range(devices)], axis=0)
+        )
+    taps[...] = terms[0].astype(jnp.float32) + terms[1].astype(jnp.float32)
+    flip = iota((LANES, LANES), 0) + iota((LANES, LANES), 1) == LANES - 1
+    flip = flip.astype(jnp.float32).astype(jnp.bfloat16)
+    taps_turned[...] = sum(
+        jnp.dot(term, flip, preferred_element_type=jnp.float32) for term in terms
+    )
     for source in range(devices):
-        rows = slice(source * SUBS, (source + 1) * SUBS)
         for field in range(3):
             place = slice(field * FIELD_ROWS, (field + 1) * FIELD_ROWS)
             both = packed_ref[source, place, :].astype(jnp.float32)
-            fields[field, 0, rows, :] = both[:SUBS]
-            fields[field, 1, rows, :] = both[SUBS:]
-        high, low = (
-            packed_ref[source, (3 + term) * FIELD_ROWS : (4 + term) * FIELD_ROWS, :].astype(
-                jnp.float32
-            )
-            for term in range(2)
-        )
-        taps[source * FIELD_ROWS : (source + 1) * FIELD_ROWS, :] = high + low
-    zeros = jnp.zeros((SUBS, LANES), jnp.float32)
+            for side in range(2):
+                rows = pl.ds(2 * source + side, SUBS, stride=blocks)
+                fields[field, rows, :] = both[side * SUBS : (side + 1) * SUBS]
+    fill_weights(packed_ref, place_ref, weight_ref, scale_ref)
+    position_sums = jnp.zeros((blocks, LANES), jnp.float32)
     for channel in range(SUBS):
-        for kind in range(4):
-            padded[channel, kind, :SUBS, :] = zeros
-            padded[channel, 4 + kind, SUBS:, :] = zeros
-    position_sums = [zeros, zeros]
-    for channel in range(SUBS):
-        strided = pl.ds(channel, devices, stride=SUBS)
-        signal, gating, probing = (
-            [fields[field, side, strided, :] for side in range(2)] for field in range(3)
-        )
-        windows_high, windows_low = [], []
-        earlier = jnp.zeros((HALF, LANES), jnp.float32)
-        for block in range(blocks):
-            row = taps[pl.ds(block * SUBS + channel, 1), :]
-            turned = pltpu.roll(
-                jnp.broadcast_to(row, (HALF, LANES)), 0, axis=1, stride=1, stride_axis=0
-            )
-            high, low = halves(jnp.where(below, earlier, turned))
-            windows_high.append(high)
-            windows_low.append(low)
-            earlier = turned
-        turned = [half_turn(vals) for vals in signal]
-        later = pltpu.roll(signal[1], 1, axis=0)
-        later_turned = pltpu.roll(turned[1], 1, axis=0)
-        later = jnp.where(row_ids == 0, 0.0, later)
-        later_turned = jnp.where(row_ids == 0, 0.0, later_turned)
-        kinds = (
-            jnp.where(low_lanes, signal[0], later_turned),
-            jnp.where(low_lanes, signal[1], turned[0]),
-            jnp.where(low_lanes, turned[0], later),
-            jnp.where(low_lanes, turned[1], signal[0]),
-        )
-        for kind in range(4):
-            padded[channel, kind, SUBS:, :] = kinds[kind]
-        left = jnp.concatenate(
-            [
-                jnp.concatenate(
-                    [padded[channel, kind, SUBS - step : 2 * SUBS - step, :] for kind in range(4)],
-                    axis=0,
-                )
-                for step in range(devices)
-            ],
-            axis=1,
-        ).astype(jnp.bfloat16)
-        right = jnp.concatenate(
-            [
-                jnp.concatenate([high, low], axis=1)
-                for high, low in zip(windows_high, windows_low)
-            ],
-            axis=0,
-        )
-        parts = jnp.dot(left, right, preferred_element_type=jnp.float32)
-        parts = parts[:, :LANES] + parts[:, LANES:]
-        even, odd = (
-            [parts[(2 * which + side) * SUBS : (2 * which + side + 1) * SUBS] for side in range(2)]
-            for which in range(2)
-        )
-        odd_before = jnp.where(row_ids == 0, 0.0, pltpu.roll(odd[1], 1, axis=0))
-        conv = (
-            even[0] + half_turn(jnp.where(low_lanes, odd[0], odd_before)),
-            even[1] + half_turn(jnp.where(low_lanes, odd[1], odd[0])),
-        )
-        back = []
-        for side in range(2):
-            mixed = gating[side] * conv[side]
-            sigmoid_val = jax.nn.sigmoid(mixed)
-            back.append(
-                gating[side] * probing[side] * sigmoid_val * (1.0 + mixed * (1.0 - sigmoid_val))
-            )
-        next_row = jnp.where(row_ids == SUBS - 1, 0.0, pltpu.roll(back[0], SUBS - 1, axis=0))
-        shifted = (
-            half_turn(jnp.where(low_lanes, back[1], back[0])),
-            half_turn(jnp.where(low_lanes, next_row, back[1])),
-        )
-        for kind, vals in enumerate((*back, *shifted)):
-            padded[channel, 4 + kind, :SUBS, :] = vals
-
-        def reach(kind, step):
-            return padded[channel, 4 + kind, step : SUBS + step, :]
-
-        pieces = []
-        for block in range(blocks):
-            step, odd_block = divmod(block, 2)
-            if odd_block:
-                group = (reach(1, step), reach(0, step + 1), reach(3, step), reach(2, step + 1))
-            else:
-                group = (reach(0, step), reach(1, step), reach(2, step), reach(3, step))
-            pieces.append(jnp.concatenate(halves(jnp.concatenate(group, axis=0)), axis=0))
-        left = jnp.concatenate(pieces, axis=1)
-        right = jnp.concatenate(
-            [jnp.concatenate(windows_high, axis=1), jnp.concatenate(windows_low, axis=1)], axis=0
-        )
-        parts = lax.dot_general(
-            left, right, (((1,), (1,)), ((), ())), preferred_element_type=jnp.float32
-        )
-        parts = parts[: 4 * SUBS] + parts[4 * SUBS :]
-        parts = parts + half_turn(parts)
-        for side in range(2):
-            grad = jnp.where(
-                low_lanes,
-                parts[side * SUBS : (side + 1) * SUBS],
-                parts[(2 + side) * SUBS : (3 + side) * SUBS],
-            )
-            saliency = grad * signal[side]
-            position_sums[side] += saliency
-            place = (channel * 2 + side) * SUBS
-            products[place : place + SUBS, :] = saliency
-    pick = (iota((SUBS, LANES), 1) // BLOCK == iota((SUBS, LANES), 0)).astype(jnp.bfloat16)
+        place = slice(channel * blocks, (channel + 1) * blocks)
+        signal, gating, probing = (fields[field, place, :] for field in range(3))
+        left = spread(signal, padded.at[channel, 0], single.at[channel, 0], -1)
+        right = windows(taps, channel, 0, lane_ids < row_ids)
+        sums = jnp.dot(left.astype(jnp.bfloat16), right, preferred_element_type=jnp.float32)
+        sums = sums[:, :LANES] + sums[:, LANES:]
+        conv = sums[:blocks]
+        for part in range(1, PARTS):
+            own = sums[part * blocks : (part + 1) * blocks]
+            wrapped = lanes >= LANES - part * PART
+            conv = conv + turn(jnp.where(wrapped, next_block(own, -1), own), part)
+        mixed = gating * conv
+        sigmoid_val = jax.nn.sigmoid(mixed)
+        back = gating * probing * sigmoid_val * (1.0 + mixed * (1.0 - sigmoid_val))
+        left = spread(back, padded.at[channel, 1], single.at[channel, 1], 1)
+        left = jnp.concatenate(halves(left), axis=0)
+        right = windows(
+            taps_turned, channel, LANES + 1 - PART, lane_ids + PART - 1 - row_ids >= LANES
+        )
+        sums = jnp.dot(left, right, preferred_element_type=jnp.float32)
+        sums = sums[:, :LANES] + sums[:, LANES:]
+        sums = sums[: PARTS * blocks] + sums[PARTS * blocks :]
+        grad = sums[(PARTS - 1) * blocks :]
+        for part in range(PARTS - 1):
+            own = sums[part * blocks : (part + 1) * blocks]
+            kept = lanes >= LANES - (part + 1) * PART
+            grad = grad + turn(jnp.where(kept, own, next_block(own, 1)), part + 1)
+        saliency = grad * signal
+        position_sums += saliency
+        products[place, :] = saliency
+    pick = iota((SUBS, LANES), 1) // BLOCK == iota((SUBS, LANES), 0)
+    pick = pick.astype(jnp.float32).astype(jnp.bfloat16)
     block_sums = sum(
         lax.dot_general(
             pick, term, (((1,), (1,)), ((), ())), preferred_element_type=jnp.float32
@@ -264,8 +255,9 @@
         for term in halves(products[...])
     )
     for device in range(devices):
-        rows = [vals[device : device + 1] for vals in position_sums] + [block_sums[:2]]
-        message = jnp.concatenate(rows, axis=0)
+        message = jnp.concatenate(
+            [position_sums[2 * device : 2 * device + 2], block_sums[:2]], axis=0
+        )
         for copy in range(copies):
             sums_ref[device * copies + copy, :, :] = message
 
@@ -303,6 +295,7 @@
     copies = lax.axis_size("ch")
     channels, length = inputs.shape
     columns = node_place.shape[0] // devices
+    blocks = devices * length // LANES
     local = (
         inputs,
         gate_values,
@@ -329,10 +322,12 @@
             jax.ShapeDtypeStruct((1, columns), jnp.float32),
         ),
         scratch_shapes=[
-            pltpu.VMEM((3, 2, devices * SUBS, LANES), jnp.float32),
-            pltpu.VMEM((devices * FIELD_ROWS, LANES), jnp.float32),
-            pltpu.VMEM((SUBS, 8, 2 * SUBS, LANES), jnp.float32),
-            pltpu.VMEM((2 * SUBS * SUBS, LANES), jnp.float32),
+            pltpu.VMEM((3, SUBS * blocks, LANES), jnp.float32),
+            pltpu.VMEM((blocks * SUBS, LANES), jnp.float32),
+            pltpu.VMEM((blocks * SUBS, LANES), jnp.float32),
+            pltpu.VMEM((SUBS, 2, 2 * blocks, LANES), jnp.float32),
+            pltpu.VMEM((SUBS, 2, PARTS, 2 * blocks, LANES), jnp.float32),
+            pltpu.VMEM((SUBS * blocks, LANES), jnp.float32),
         ],
         compiler_params=LEAN,
         name="saliency",

time: 31.9 us -> 30.7 us (0.962)
  Pallas kernels: 5.56 us -> 4.39 us
    pallas_call x1, Pallas kernels: 3.56 us -> 2.38 us  [whole_channels(): pl.pallas_call(saliency_kernel, out_shape=(jax.ShapeDtypeStruct((devices...]
where the time goes in v2:
time: 30.7 us; the launch traced here: 30.5 us
  blocking collectives  25.4 us (83%)
  Pallas kernels  4.39 us (14%)
  between operations  0.66 us (2%)
    all_to_all x1, blocking collectives, whole_channels(): lax.all_to_all(packed, 'seq', split_axis=0, concat_axis=0, tiled=True)  15 us
    all_to_all x1, blocking collectives, whole_channels(): lax.all_to_all(sums, ('seq', 'ch'), split_axis=0, concat_axis=0, tiled=True)  10.4 us
    pallas_call x1, Pallas kernels, whole_channels(): pl.pallas_call(saliency_kernel, out_shape=(jax.ShapeDtypeStruct((devices...  2.38 us
    pallas_call x1, Pallas kernels, whole_channels(): pl.pallas_call(functools.partial(pack_kernel, length // BLOCK), out_shape...  1.07 us
    pallas_call x1, Pallas kernels, whole_channels(): pl.pallas_call(functools.partial(finish_kernel, channels * copies), out_s...  0.94 us

profile of v2, /device:TPU:0, one launch (start us, length us, event | category | flops | bytes accessed | tf_op | source)
XLA Modules:
  0.0 30.5 jit_solution(10365475689805965789)
XLA Ops:
  0.6 1.1 %pack.1 = bf16[8,96,128]{2,1,0:T(8,128)(2,1)S(1)} custom-call(bf16[64,256]{1,0:T(8,128)(2,1)} %refs_0_.1, bf16[64,256]{1,0:T(8,128)(2,1)} %refs_1_.1, bf16[64,256]{1,0:T(8,128)(2,1)} %refs_2_.1, f32[64,256]{1,0:T(8,128)} %refs_3_.1, s32[1,8]{1,0:T(1,128)} %bitcast.5, s32[1,8]{1,0:T(1,128)} %bitcast.6), custom_call_target="tpu_custom_call" | custom-call | tf_op jit(solution)/shard_map/pack/pallas_call | solution.py:307
  1.7 0.0 copy-start
  1.7 15.0 %all_to_all.10.packed_ref = bf16[8,96,128]{2,1,0:T(8,128)(2,1)S(1)} all-to-all(bf16[8,96,128]{2,1,0:T(8,128)(2,1)S(1)} %pack.1), channel_id=1, replica_groups=mesh['seq'=8,'ch'=4] {'seq'}, dimensions={0} | all-to-all | bytes 393216 | tf_op jit(solution)/shard_map/all_to_all | solution.py:316
  16.7 0.0 copy-done
  16.8 2.4 %saliency.1 = (f32[32,4,128]{2,1,0:T(4,128)S(1)}, bf16[256,1024]{1,0:T(8,128)(2,1)S(1)}, f32[1,1024]{1,0:T(1,128)S(1)}) custom-call(bf16[8,96,128]{2,1,0:T(8,128)(2,1)S(1)} %all_to_all.10.packed_ref, s32[64,128]{1,0:T(8,128)S(1)} %bitcast.4), custom_call_target="tpu_custom_call" | custom-call | tf_op jit(solution)/shard_map/saliency/pallas_call | solution.py:317
  19.1 10.4 %all_to_all.11.sums_ref = f32[32,4,128]{2,1,0:T(4,128)S(1)} all-to-all(f32[32,4,128]{2,1,0:T(4,128)S(1)} %get-tuple-element.7), channel_id=1, replica_groups=mesh['seq'=8,'ch'=4] {'seq','ch'}, dimensions={0} | all-to-all | bytes 131072 | tf_op jit(solution)/shard_map/all_to_all | solution.py:335
  29.5 0.9 %finish.1 = (f32[2,128]{1,0:T(2,128)}, f32[64,1024]{1,0:T(8,128)}) custom-call(f32[32,4,128]{2,1,0:T(4,128)S(1)} %all_to_all.11.sums_ref, bf16[256,1024]{1,0:T(8,128)(2,1)S(1)} %get-tuple-element.8.weight_ref, f32[1,1024]{1,0:T(1,128)S(1)} %get-tuple-element.9.scale_ref), custom_call_target="tpu_custom_call" | custom-call | tf_op jit(solution)/shard_map/finish/pallas_call | solution.py:336
Async XLA Ops:
  1.7 15.0 %copy-start = (s32[8192]{0:T(1024)S(1)}, s32[8192]{0:T(1024)}, u32[]{:S(2)}) copy-start(s32[8192]{0:T(1024)} %param.13) | copy-start | bytes 98308

commit v3 on v2

--- a/solution.py
+++ b/solution.py
@@ -17,8 +17,7 @@
 PARTS = LANES // PART
 FIELD_ROWS = 16
 FIELDS = 5
-MEMBER_ROW = FIELDS * FIELD_ROWS
-PACK_ROWS = MEMBER_ROW + FIELD_ROWS
+PACK_ROWS = FIELDS * FIELD_ROWS
 
 
 HIGHEST = lax.Precision.HIGHEST
@@ -34,18 +33,48 @@
     return high, (vals - high.astype(jnp.float32)).astype(jnp.bfloat16)
 
 
-def pack_kernel(blocks_dev, *refs):
-    sources, packed_ref, arrived, landed = refs[:6], refs[6], refs[7:13], refs[13]
-    inputs_ref, gate_ref, probe_ref, taps_ref, blocks_ref, nodes_ref = arrived
-    devices = packed_ref.shape[0]
+def as_column(row, count):
+    width = row.shape[1]
+    same = iota((count, width), 0) == iota((count, width), 1)
+    return jnp.sum(jnp.where(same, row, 0.0), axis=1, keepdims=True)
+
+
+def member_rows(blocks_ref, nodes_ref, place_ref):
+    nodes = nodes_ref[...]
+    count = nodes.shape[1]
+    place = place_ref[...]
+    row_pick = as_column((nodes // LANES).astype(jnp.float32), count) == iota(
+        (count, place.shape[0]), 1
+    ).astype(jnp.float32)
+    row_pick = row_pick.astype(jnp.float32).astype(jnp.bfloat16)
+    high, low = (
+        jnp.dot(
+            row_pick,
+            digit.astype(jnp.float32).astype(jnp.bfloat16),
+            preferred_element_type=jnp.float32,
+        )
+        for digit in (place // LANES, place % LANES)
+    )
+    lanes = iota((count, LANES), 1)
+    low_digit = as_column((nodes % LANES).astype(jnp.float32), count)
+    found = jnp.where(lanes.astype(jnp.float32) == low_digit, high * LANES + low, 0.0)
+    targets = jnp.sum(found, axis=1, keepdims=True)
+    blocks = as_column(blocks_ref[...].astype(jnp.float32), count)
+    own = lanes == iota((count, LANES), 0) + lax.axis_index("seq") * count
+    return jnp.concatenate(
+        [jnp.sum(jnp.where(own, vals, 0.0), axis=0, keepdims=True) for vals in (targets, blocks)],
+        axis=0,
+    )
+
+
+def pack_kernel(*refs):
+    sources, (packed_ref, members_ref), arrived, landed = refs[:7], refs[7:9], refs[9:16], refs[16]
     loads = [
         pltpu.make_async_copy(source, target, landed.at[place])
         for place, (source, target) in enumerate(zip(sources, arrived))
     ]
-    for load in loads:
+    for load in loads[4:] + loads[:4]:
         load.start()
-    for load in loads:
-        load.wait()
 
     def put(pair, field, tiles):
         for side in range(2):
@@ -54,91 +83,32 @@
             place = slice(field * FIELD_ROWS, (field + 1) * FIELD_ROWS)
             packed_ref[2 * pair + side, place, :] = both.astype(jnp.bfloat16)
 
-    for pair in range(devices // 2):
-        rows = slice(pair * 2 * SUBS, (pair + 1) * 2 * SUBS)
-        columns = [slice(0, LANES), slice(LANES, 2 * LANES)]
-        for field, ref in enumerate((inputs_ref, gate_ref, probe_ref)):
-            put(pair, field, [ref[rows, cols].astype(jnp.float32) for cols in columns])
-        split = [halves(taps_ref[rows, cols]) for cols in columns]
-        for term in range(2):
-            put(pair, 3 + term, [terms[term].astype(jnp.float32) for terms in split])
-
-    def as_column(row):
-        members = row.shape[1]
-        same = iota((members, members), 0) == iota((members, members), 1)
-        return jnp.sum(jnp.where(same, row, 0).astype(jnp.float32), axis=1, keepdims=True)
-
-    nodes = nodes_ref[...]
-    low_lanes = iota((SUBS, LANES), 1) < HALF
-    digits = jnp.where(low_lanes, as_column(nodes // LANES), as_column(nodes % LANES))
-    places = jnp.broadcast_to(as_column(blocks_ref[...] % blocks_dev), (SUBS, LANES))
-    member_rows = jnp.concatenate([digits, places], axis=0).astype(jnp.bfloat16)
-    for device in range(devices):
-        packed_ref[device, MEMBER_ROW:, :] = member_rows
-
-
-def fill_weights(packed_ref, place_ref, weight_ref, scale_ref):
-    devices = packed_ref.shape[0]
-    members = devices * SUBS
-    columns = weight_ref.shape[1]
-    blocks_dev = 2 * LANES // BLOCK
-    digits, offsets = [], []
-    for source in range(devices):
-        both = packed_ref[source, MEMBER_ROW:, :].astype(jnp.float32)
-        digits.append(both[:SUBS])
-        offsets.append(both[SUBS:] + float(source * blocks_dev))
-    digits = jnp.concatenate(digits, axis=0)
-    offsets = jnp.concatenate(offsets, axis=0)
-    place = place_ref[...]
-    place_rows = place.shape[0]
-    row_pick = iota((members, place_rows), 1).astype(jnp.float32) == digits[:, :1]
-    row_pick = row_pick.astype(jnp.bfloat16)
-    lane_ids = iota((members, LANES), 1).astype(jnp.float32)
-    low_digit = jnp.broadcast_to(digits[:, HALF : HALF + 1], (members, LANES))
-
-    def looked_up(table):
-        found = jnp.dot(
-            row_pick, table.astype(jnp.float32).astype(jnp.bfloat16),
-            preferred_element_type=jnp.float32,
-        )
-        return jnp.sum(jnp.where(lane_ids == low_digit, found, 0.0), axis=1, keepdims=True)
-
-    targets = looked_up(place // LANES) * LANES + looked_up(place % LANES)
-    targets = targets - (lax.axis_index("seq") * columns).astype(jnp.float32)
-    node_pick = iota((members, columns), 1).astype(jnp.float32) == targets
-    node_pick = node_pick.astype(jnp.float32)
-    counts = jnp.sum(node_pick, axis=0, keepdims=True)
-    scale_ref[...] = 1.0 / jnp.maximum(counts, 1.0)
-    slot = iota((members, 2 * LANES), 1)
-    slot_block = slot % (2 * SUBS) * 2 + slot // LANES
-    own_block = jnp.broadcast_to(offsets[:, :1], (members, 2 * LANES))
-    block_pick = (slot_block.astype(jnp.float32) == own_block).astype(jnp.float32)
-    weight_ref[...] = lax.dot_general(
-        block_pick.T.astype(jnp.bfloat16),
-        node_pick.astype(jnp.bfloat16),
-        (((1,), (0,)), ((), ())),
-        preferred_element_type=jnp.float32,
-    ).astype(jnp.bfloat16)
-
-
-def windows(taps, channel, first_turn, from_earlier):
+    for load in loads[4:]:
+        load.wait()
+    members_ref[...] = member_rows(*arrived[4:])
+    columns = [slice(0, LANES), slice(LANES, 2 * LANES)]
+    for field in range(4):
+        loads[field].wait()
+        for pair in range(packed_ref.shape[0] // 2):
+            rows = slice(pair * 2 * SUBS, (pair + 1) * 2 * SUBS)
+            tiles = [arrived[field][rows, cols] for cols in columns]
+            if field < 3:
+                put(pair, field, [tile.astype(jnp.float32) for tile in tiles])
+                continue
+            split = [halves(tile) for tile in tiles]
+            for term in range(2):
+                put(pair, field + term, [terms[term].astype(jnp.float32) for terms in split])
+
+
+def windows(row_of, blocks, first_turn, from_earlier):
     rows = []
     earlier = jnp.zeros((PART, LANES), jnp.float32)
-    for block in range(taps.shape[0] // SUBS):
-        row = jnp.broadcast_to(taps[pl.ds(block * SUBS + channel, 1), :], (PART, LANES))
+    for block in range(blocks):
+        row = jnp.broadcast_to(row_of(block), (PART, LANES))
         turned = pltpu.roll(row, first_turn, axis=1, stride=1, stride_axis=0)
-        rows.append(jnp.concatenate(halves(jnp.where(from_earlier, earlier, turned)), axis=1))
+        rows.append(jnp.where(from_earlier, earlier, turned))
         earlier = turned
-    return jnp.concatenate(rows, axis=0)
-
-
-def by_part(pieces):
-    blocks = pieces[0].shape[0]
-    lanes = iota((blocks, LANES), 1)
-    result = pieces[-1]
-    for part in range(len(pieces) - 2, -1, -1):
-        result = jnp.where(lanes < (part + 1) * PART, pieces[part], result)
-    return result
+    return rows
 
 
 def turn(vals, parts):
@@ -146,17 +116,41 @@
     return pltpu.roll(vals, shift, axis=1) if shift else vals
 
 
-def spread(rows, padded, single, sign):
+def exchanged(pieces):
+    lanes = iota(pieces[0].shape, 1)
+    low = lanes < 2 * PART
+    crossed = [None] * PARTS
+    for place in range(2):
+        first, second = pieces[place], pieces[place + 2]
+        swapped = turn(jnp.where(low, second, first), 2)
+        crossed[place] = jnp.where(low, first, swapped)
+        crossed[place + 2] = jnp.where(low, swapped, second)
+    even = lanes % (2 * PART) < PART
+    result = []
+    for first, second in (crossed[:2], crossed[2:]):
+        result.append(jnp.where(even, first, turn(second, 1)))
+        result.append(jnp.where(even, turn(first, -1), second))
+    return result
+
+
+def joined_parts(rows, single, sign):
     blocks = rows.shape[0]
     start = blocks if sign < 0 else 0
-    zeros = jnp.zeros((blocks, LANES), jnp.float32)
     single[start : start + blocks, :] = rows
-    single[blocks - start : 2 * blocks - start, :] = zeros
-    moved = [single[start + sign * step : start + sign * step + blocks, :] for step in range(PARTS)]
+    single[blocks - start : 2 * blocks - start, :] = jnp.zeros((blocks, LANES), jnp.float32)
+    return exchanged(
+        [single[start + sign * step : start + sign * step + blocks, :] for step in range(PARTS)]
+    )
+
+
+def spread(joined, padded, sign):
+    blocks = joined[0].shape[0]
+    start = blocks if sign < 0 else 0
     for part in range(PARTS):
-        joined = by_part([turn(moved[step], step - part) for step in range(PARTS)])
-        padded[part, start : start + blocks, :] = joined
-        padded[part, blocks - start : 2 * blocks - start, :] = zeros
+        padded[part, start : start + blocks, :] = joined[part]
+        padded[part, blocks - start : 2 * blocks - start, :] = jnp.zeros(
+            (blocks, LANES), jnp.float32
+        )
     columns = []
     for step in range(0, blocks, PARTS):
         offset = start + sign * step
@@ -165,7 +159,7 @@
                 [padded[part, offset : offset + blocks, :] for part in range(PARTS)], axis=0
             )
         )
-    return jnp.concatenate(columns, axis=1)
+    return jnp.concatenate(columns, axis=1).astype(jnp.bfloat16)
 
 
 def next_block(vals, sign):
@@ -178,12 +172,9 @@
 
 def saliency_kernel(
     packed_ref,
-    place_ref,
+    members_ref,
     sums_ref,
-    weight_ref,
-    scale_ref,
     fields,
-    taps,
     taps_turned,
     single,
     padded,
@@ -200,28 +191,41 @@
         terms.append(
             jnp.concatenate([packed_ref[source, place, :] for source in range(devices)], axis=0)
         )
-    taps[...] = terms[0].astype(jnp.float32) + terms[1].astype(jnp.float32)
     flip = iota((LANES, LANES), 0) + iota((LANES, LANES), 1) == LANES - 1
     flip = flip.astype(jnp.float32).astype(jnp.bfloat16)
     taps_turned[...] = sum(
         jnp.dot(term, flip, preferred_element_type=jnp.float32) for term in terms
     )
     for source in range(devices):
-        for field in range(3):
+        for field in range(FIELDS):
             place = slice(field * FIELD_ROWS, (field + 1) * FIELD_ROWS)
             both = packed_ref[source, place, :].astype(jnp.float32)
             for side in range(2):
                 rows = pl.ds(2 * source + side, SUBS, stride=blocks)
                 fields[field, rows, :] = both[side * SUBS : (side + 1) * SUBS]
-    fill_weights(packed_ref, place_ref, weight_ref, scale_ref)
     position_sums = jnp.zeros((blocks, LANES), jnp.float32)
     for channel in range(SUBS):
         place = slice(channel * blocks, (channel + 1) * blocks)
-        signal, gating, probing = (fields[field, place, :] for field in range(3))
-        left = spread(signal, padded.at[channel, 0], single.at[channel, 0], -1)
-        right = windows(taps, channel, 0, lane_ids < row_ids)
-        sums = jnp.dot(left.astype(jnp.bfloat16), right, preferred_element_type=jnp.float32)
-        sums = sums[:, :LANES] + sums[:, LANES:]
+        signal, gating, probing, *filters = (fields[field, place, :] for field in range(FIELDS))
+        left = jnp.concatenate(
+            [
+                spread(
+                    joined_parts(filters[term], single.at[channel, term], -1),
+                    padded.at[channel, term],
+                    -1,
+                )
+                for term in range(2)
+            ],
+            axis=0,
+        )
+
+        def signal_row(block, first=channel * blocks):
+            return fields[0, first + block : first + block + 1, :]
+
+        right = windows(signal_row, blocks, 0, lane_ids < row_ids)
+        right = jnp.concatenate([rows.astype(jnp.bfloat16) for rows in right], axis=0)
+        sums = jnp.dot(left, right, preferred_element_type=jnp.float32)
+        sums = sums[: PARTS * blocks] + sums[PARTS * blocks :]
         conv = sums[:blocks]
         for part in range(1, PARTS):
             own = sums[part * blocks : (part + 1) * blocks]
@@ -230,10 +234,25 @@
         mixed = gating * conv
         sigmoid_val = jax.nn.sigmoid(mixed)
         back = gating * probing * sigmoid_val * (1.0 + mixed * (1.0 - sigmoid_val))
-        left = spread(back, padded.at[channel, 1], single.at[channel, 1], 1)
-        left = jnp.concatenate(halves(left), axis=0)
+        joined = joined_parts(back, single.at[channel, 2], 1)
+        high = [vals.astype(jnp.bfloat16).astype(jnp.float32) for vals in joined]
+        low = [vals - term for vals, term in zip(joined, high)]
+        left = jnp.concatenate(
+            [
+                spread(vals, padded.at[channel, 2 + term], 1)
+                for term, vals in enumerate((high, low))
+            ],
+            axis=0,
+        )
+
+        def filter_row(block, first=channel):
+            return taps_turned[block * SUBS + first : block * SUBS + first + 1, :]
+
         right = windows(
-            taps_turned, channel, LANES + 1 - PART, lane_ids + PART - 1 - row_ids >= LANES
+            filter_row, blocks, LANES + 1 - PART, lane_ids + PART - 1 - row_ids >= LANES
+        )
+        right = jnp.concatenate(
+            [jnp.concatenate(halves(rows), axis=1) for rows in right], axis=0
         )
         sums = jnp.dot(left, right, preferred_element_type=jnp.float32)
         sums = sums[:, :LANES] + sums[:, LANES:]
@@ -254,38 +273,58 @@
         )
         for term in halves(products[...])
     )
-    for device in range(devices):
-        message = jnp.concatenate(
-            [position_sums[2 * device : 2 * device + 2], block_sums[:2]], axis=0
-        )
-        for copy in range(copies):
-            sums_ref[device * copies + copy, :, :] = message
-
-
-def finish_kernel(channel_count, sums_ref, weight_ref, scale_ref, position_ref, nodes_ref):
+    own = lax.axis_index("ch")
+    for copy in range(copies):
+        rest = jnp.where(own == copy, block_sums[:2], members_ref[...])
+        for device in range(devices):
+            sums_ref[copy * devices + device, :, :] = jnp.concatenate(
+                [position_sums[2 * device : 2 * device + 2], rest], axis=0
+            )
+
+
+def finish_kernel(members, channel_count, sums_ref, position_ref, nodes_ref):
     copies = lax.axis_size("ch")
     devices = sums_ref.shape[0] // copies
+    columns = nodes_ref.shape[1]
     own = lax.axis_index("ch")
     total = sums_ref[0]
     for source in range(1, devices * copies):
         total = total + sums_ref[source]
     position_ref[...] = total[:2] / channel_count
+    other = lax.rem(own + 1, copies) * devices
+    listed = sums_ref[other]
+    for source in range(1, devices):
+        listed = listed + sums_ref[other + source]
+    targets = as_column(listed[2:3], members)
+    targets = targets - (lax.axis_index("seq") * columns).astype(jnp.float32)
+    node_pick = iota((members, columns), 1).astype(jnp.float32) == targets
+    node_pick = node_pick.astype(jnp.float32)
+    scale = 1.0 / jnp.maximum(jnp.sum(node_pick, axis=0, keepdims=True), 1.0)
+    slot = iota((2 * LANES, LANES), 0)
+    slot_block = (slot % (2 * SUBS) * 2 + slot // LANES).astype(jnp.float32)
+    block_pick = (slot_block == listed[3:4]).astype(jnp.float32).astype(jnp.bfloat16)
     own_lanes = iota((SUBS, LANES), 1) // (2 * SUBS) == iota((SUBS, LANES), 0)
     rows = []
     for source in range(devices):
-        message = sums_ref[source * copies + own]
+        message = sums_ref[own * devices + source]
         rows.append(
             jnp.concatenate(
                 [jnp.where(own_lanes, message[2 + side : 3 + side], 0.0) for side in range(2)],
                 axis=1,
             )
         )
-    high, low = halves(jnp.concatenate(rows, axis=0))
+    picked = jnp.dot(
+        jnp.concatenate(halves(jnp.concatenate(rows, axis=0)), axis=0),
+        block_pick[:, :members],
+        preferred_element_type=jnp.float32,
+    )
     both = jnp.dot(
-        jnp.concatenate([high, low], axis=0), weight_ref[...], preferred_element_type=jnp.float32
-    )
-    count = high.shape[0]
-    nodes_ref[...] = (both[:count] + both[count:]) * scale_ref[...]
+        picked.astype(jnp.bfloat16),
+        node_pick.astype(jnp.bfloat16),
+        preferred_element_type=jnp.float32,
+    )
+    count = devices * SUBS
+    nodes_ref[...] = (both[:count] + both[count:]) * scale
 
 
 def whole_channels(
@@ -303,10 +342,14 @@
         filter_taps,
         member_blocks.reshape(1, -1),
         member_nodes.reshape(1, -1),
-    )
-    packed = pl.pallas_call(
-        functools.partial(pack_kernel, length // BLOCK),
-        out_shape=jax.ShapeDtypeStruct((devices, PACK_ROWS, LANES), jnp.bfloat16),
+        node_place.reshape(-1, LANES),
+    )
+    packed, members = pl.pallas_call(
+        pack_kernel,
+        out_shape=(
+            jax.ShapeDtypeStruct((devices, PACK_ROWS, LANES), jnp.bfloat16),
+            jax.ShapeDtypeStruct((2, LANES), jnp.float32),
+        ),
         in_specs=[pl.BlockSpec(memory_space=pltpu.HBM)] * len(local),
         scratch_shapes=[pltpu.VMEM(part.shape, part.dtype) for part in local]
         + [pltpu.SemaphoreType.DMA((len(local),))],
@@ -314,34 +357,29 @@
         name="pack",
     )(*(pltpu.with_memory_space_constraint(part, pltpu.HBM) for part in local))
     packed = lax.all_to_all(packed, "seq", split_axis=0, concat_axis=0, tiled=True)
-    sums, weight, scale = pl.pallas_call(
+    sums = pl.pallas_call(
         saliency_kernel,
-        out_shape=(
-            jax.ShapeDtypeStruct((devices * copies, 4, LANES), jnp.float32),
-            jax.ShapeDtypeStruct((2 * LANES, columns), jnp.bfloat16),
-            jax.ShapeDtypeStruct((1, columns), jnp.float32),
-        ),
+        out_shape=jax.ShapeDtypeStruct((devices * copies, 4, LANES), jnp.float32),
         scratch_shapes=[
-            pltpu.VMEM((3, SUBS * blocks, LANES), jnp.float32),
+            pltpu.VMEM((FIELDS, SUBS * blocks, LANES), jnp.float32),
             pltpu.VMEM((blocks * SUBS, LANES), jnp.float32),
-            pltpu.VMEM((blocks * SUBS, LANES), jnp.float32),
-            pltpu.VMEM((SUBS, 2, 2 * blocks, LANES), jnp.float32),
-            pltpu.VMEM((SUBS, 2, PARTS, 2 * blocks, LANES), jnp.float32),
+            pltpu.VMEM((SUBS, 3, 2 * blocks, LANES), jnp.float32),
+            pltpu.VMEM((SUBS, 4, PARTS, 2 * blocks, LANES), jnp.float32),
             pltpu.VMEM((SUBS * blocks, LANES), jnp.float32),
         ],
         compiler_params=LEAN,
         name="saliency",
-    )(packed, node_place.reshape(-1, LANES))
-    sums = lax.all_to_all(sums, ("seq", "ch"), split_axis=0, concat_axis=0, tiled=True)
+    )(packed, members)
+    sums = lax.all_to_all(sums, ("ch", "seq"), split_axis=0, concat_axis=0, tiled=True)
     position, node_rows = pl.pallas_call(
-        functools.partial(finish_kernel, channels * copies),
+        functools.partial(finish_kernel, devices * member_nodes.shape[0], channels * copies),
         out_shape=(
             jax.ShapeDtypeStruct((2, LANES), jnp.float32),
             jax.ShapeDtypeStruct((channels, columns), jnp.float32),
         ),
         compiler_params=LEAN,
         name="finish",
-    )(sums, weight, scale)
+    )(sums)
     return position.reshape(length), node_rows
 
 

time: 30.7 us -> 30 us (0.977)
  blocking collectives: 25.4 us -> 24.6 us
    all_to_all x1, blocking collectives: 10.4 us -> 9.94 us  [whole_channels(): lax.all_to_all(sums, ('ch', 'seq'), split_axis=0, concat_axis=0, tiled=True)]
    all_to_all x1, blocking collectives: 15 us -> 14.6 us  [whole_channels(): lax.all_to_all(packed, 'seq', split_axis=0, concat_axis=0, tiled=True)]
where the time goes in v3:
time: 30 us; the launch traced here: 29.8 us
  blocking collectives  24.6 us (82%)
  Pallas kernels  4.54 us (15%)
  between operations  0.65 us (2%)
    all_to_all x1, blocking collectives, whole_channels(): lax.all_to_all(packed, 'seq', split_axis=0, concat_axis=0, tiled=True)  14.6 us
    all_to_all x1, blocking collectives, whole_channels(): lax.all_to_all(sums, ('ch', 'seq'), split_axis=0, concat_axis=0, tiled=True)  9.94 us
    pallas_call x1, Pallas kernels, whole_channels(): pl.pallas_call(saliency_kernel, out_shape=jax.ShapeDtypeStruct((devices *...  2.28 us
    pallas_call x1, Pallas kernels, whole_channels(): pl.pallas_call(pack_kernel, out_shape=(jax.ShapeDtypeStruct((devices, PAC...  1.17 us
    pallas_call x1, Pallas kernels, whole_channels(): pl.pallas_call(functools.partial(finish_kernel, devices * member_nodes.sh...  1.09 us

profile of v3, /device:TPU:0, one launch (start us, length us, event | category | flops | bytes accessed | tf_op | source)
XLA Modules:
  0.0 29.8 jit_solution(1098407981969922506)
XLA Ops:
  0.6 1.2 %pack.1 = (bf16[8,80,128]{2,1,0:T(8,128)(2,1)S(1)}, f32[2,128]{1,0:T(2,128)S(1)}) custom-call(bf16[64,256]{1,0:T(8,128)(2,1)} %refs_0_.1, bf16[64,256]{1,0:T(8,128)(2,1)} %refs_1_.1, bf16[64,256]{1,0:T(8,128)(2,1)} %refs_2_.1, f32[64,256]{1,0:T(8,128)} %refs_3_.1, s32[1,8]{1,0:T(1,128)} %bitcast.5, s32[1,8]{1,0:T(1,128)} %bitcast.6, s32[64,128]{1,0:T(8,128)} %bitcast.4), custom_call_target="tpu_custom_call" | custom-call | tf_op jit(solution)/shard_map/pack/pallas_call | solution.py:347
  1.8 14.6 %all_to_all.10.packed_ref = bf16[8,80,128]{2,1,0:T(8,128)(2,1)S(1)} all-to-all(bf16[8,80,128]{2,1,0:T(8,128)(2,1)S(1)} %get-tuple-element.6), channel_id=1, replica_groups=mesh['seq'=8,'ch'=4] {'seq'}, dimensions={0} | all-to-all | bytes 327680 | tf_op jit(solution)/shard_map/all_to_all | solution.py:359
  16.5 2.3 %saliency.1 = f32[32,4,128]{2,1,0:T(4,128)S(1)} custom-call(bf16[8,80,128]{2,1,0:T(8,128)(2,1)S(1)} %all_to_all.10.packed_ref, f32[2,128]{1,0:T(2,128)S(1)} %get-tuple-element.7.members_ref), custom_call_target="tpu_custom_call" | custom-call | tf_op jit(solution)/shard_map/saliency/pallas_call | solution.py:360
  18.7 9.9 %all_to_all.11.sums_ref = f32[32,4,128]{2,1,0:T(4,128)S(1)} all-to-all(f32[32,4,128]{2,1,0:T(4,128)S(1)} %saliency.1), channel_id=1, replica_groups=mesh['seq'=8,'ch'=4] {'ch','seq'}, dimensions={0} | all-to-all | bytes 131072 | tf_op jit(solution)/shard_map/all_to_all | solution.py:373
  28.7 1.1 %finish.1 = (f32[2,128]{1,0:T(2,128)}, f32[64,1024]{1,0:T(8,128)}) custom-call(f32[32,4,128]{2,1,0:T(4,128)S(1)} %all_to_all.11.sums_ref), custom_call_target="tpu_custom_call" | custom-call | tf_op jit(solution)/shard_map/finish/pallas_call | solution.py:374

commit v4 on v3

--- a/solution.py
+++ b/solution.py
@@ -68,12 +68,14 @@
 
 
 def pack_kernel(*refs):
-    sources, (packed_ref, members_ref), arrived, landed = refs[:7], refs[7:9], refs[9:16], refs[16]
+    sources, packed_ref, lists, arrived, landed = (
+        refs[:7], refs[7], refs[8:11], refs[11:15], refs[15]
+    )
     loads = [
         pltpu.make_async_copy(source, target, landed.at[place])
-        for place, (source, target) in enumerate(zip(sources, arrived))
+        for place, (source, target) in enumerate(zip(sources, (*arrived, *lists)))
     ]
-    for load in loads[4:] + loads[:4]:
+    for load in loads:
         load.start()
 
     def put(pair, field, tiles):
@@ -83,9 +85,6 @@
             place = slice(field * FIELD_ROWS, (field + 1) * FIELD_ROWS)
             packed_ref[2 * pair + side, place, :] = both.astype(jnp.bfloat16)
 
-    for load in loads[4:]:
-        load.wait()
-    members_ref[...] = member_rows(*arrived[4:])
     columns = [slice(0, LANES), slice(LANES, 2 * LANES)]
     for field in range(4):
         loads[field].wait()
@@ -99,16 +98,20 @@
             for term in range(2):
                 put(pair, field + term, [terms[term].astype(jnp.float32) for terms in split])
 
-
-def windows(row_of, blocks, first_turn, from_earlier):
+    for load in loads[4:]:
+        load.wait()
+
+
+def windows(taps, first, blocks):
+    later = iota((PART, LANES), 1) >= iota((PART, LANES), 0)
     rows = []
     earlier = jnp.zeros((PART, LANES), jnp.float32)
     for block in range(blocks):
-        row = jnp.broadcast_to(row_of(block), (PART, LANES))
-        turned = pltpu.roll(row, first_turn, axis=1, stride=1, stride_axis=0)
-        rows.append(jnp.where(from_earlier, earlier, turned))
+        row = jnp.broadcast_to(taps[first + block : first + block + 1, :], (PART, LANES))
+        turned = pltpu.roll(row, 0, axis=1, stride=1, stride_axis=0)
+        rows.append(jnp.concatenate(halves(jnp.where(later, turned, earlier)), axis=1))
         earlier = turned
-    return rows
+    return jnp.concatenate(rows, axis=0)
 
 
 def turn(vals, parts):
@@ -162,6 +165,14 @@
     return jnp.concatenate(columns, axis=1).astype(jnp.bfloat16)
 
 
+def spread_terms(joined, padded, sign):
+    high = [vals.astype(jnp.bfloat16).astype(jnp.float32) for vals in joined]
+    low = [vals - term for vals, term in zip(joined, high)]
+    return jnp.concatenate(
+        [spread(vals, ref, sign) for vals, ref in zip((high, low), padded)], axis=0
+    )
+
+
 def next_block(vals, sign):
     blocks = vals.shape[0]
     row_ids = iota((blocks, LANES), 0)
@@ -170,102 +181,88 @@
     return jnp.where(row_ids == blocks - 1, 0.0, pltpu.roll(vals, blocks - 1, axis=0))
 
 
+def overlapped(sums, sign):
+    blocks = sums.shape[0] // PARTS
+    lanes = iota((blocks, LANES), 1)
+    result = sums[:blocks]
+    for part in range(1, PARTS):
+        own = sums[part * blocks : (part + 1) * blocks]
+        wrapped = lanes >= LANES - part * PART
+        result = result + turn(jnp.where(wrapped, next_block(own, sign), own), part)
+    return result
+
+
 def saliency_kernel(
     packed_ref,
-    members_ref,
+    blocks_ref,
+    nodes_ref,
+    place_ref,
     sums_ref,
     fields,
-    taps_turned,
     single,
     padded,
     products,
+    held,
 ):
     devices = packed_ref.shape[0]
     blocks = 2 * devices
     copies = sums_ref.shape[0] // devices
-    row_ids, lane_ids = iota((PART, LANES), 0), iota((PART, LANES), 1)
-    lanes = iota((blocks, LANES), 1)
-    terms = []
-    for term in range(2):
-        place = slice((3 + term) * FIELD_ROWS, (4 + term) * FIELD_ROWS)
-        terms.append(
-            jnp.concatenate([packed_ref[source, place, :] for source in range(devices)], axis=0)
-        )
+    for source in range(devices):
+        rows = [
+            packed_ref[source, field * FIELD_ROWS : (field + 1) * FIELD_ROWS, :].astype(jnp.float32)
+            for field in range(FIELDS)
+        ]
+        rows = [*rows[:3], rows[3] + rows[4]]
+        for field in range(4):
+            for side in range(2):
+                place = pl.ds(2 * source + side, SUBS, stride=blocks)
+                fields[field, place, :] = rows[field][side * SUBS : (side + 1) * SUBS]
     flip = iota((LANES, LANES), 0) + iota((LANES, LANES), 1) == LANES - 1
     flip = flip.astype(jnp.float32).astype(jnp.bfloat16)
-    taps_turned[...] = sum(
-        jnp.dot(term, flip, preferred_element_type=jnp.float32) for term in terms
-    )
-    for source in range(devices):
-        for field in range(FIELDS):
-            place = slice(field * FIELD_ROWS, (field + 1) * FIELD_ROWS)
-            both = packed_ref[source, place, :].astype(jnp.float32)
-            for side in range(2):
-                rows = pl.ds(2 * source + side, SUBS, stride=blocks)
-                fields[field, rows, :] = both[side * SUBS : (side + 1) * SUBS]
+    flip_both = jnp.concatenate([flip, flip], axis=0)
+
+    def flipped(vals):
+        return jnp.dot(
+            jnp.concatenate(halves(vals), axis=1), flip_both, preferred_element_type=jnp.float32
+        )
+
+    fields[4] = jnp.dot(
+        fields[0].astype(jnp.bfloat16), flip, preferred_element_type=jnp.float32
+    )
+    members = member_rows(blocks_ref, nodes_ref, place_ref)
     position_sums = jnp.zeros((blocks, LANES), jnp.float32)
+    backs = []
     for channel in range(SUBS):
         place = slice(channel * blocks, (channel + 1) * blocks)
-        signal, gating, probing, *filters = (fields[field, place, :] for field in range(FIELDS))
-        left = jnp.concatenate(
-            [
-                spread(
-                    joined_parts(filters[term], single.at[channel, term], -1),
-                    padded.at[channel, term],
-                    -1,
-                )
-                for term in range(2)
-            ],
-            axis=0,
-        )
-
-        def signal_row(block, first=channel * blocks):
-            return fields[0, first + block : first + block + 1, :]
-
-        right = windows(signal_row, blocks, 0, lane_ids < row_ids)
-        right = jnp.concatenate([rows.astype(jnp.bfloat16) for rows in right], axis=0)
-        sums = jnp.dot(left, right, preferred_element_type=jnp.float32)
-        sums = sums[: PARTS * blocks] + sums[PARTS * blocks :]
-        conv = sums[:blocks]
-        for part in range(1, PARTS):
-            own = sums[part * blocks : (part + 1) * blocks]
-            wrapped = lanes >= LANES - part * PART
-            conv = conv + turn(jnp.where(wrapped, next_block(own, -1), own), part)
+        signal, gating, probing = (fields[field, place, :] for field in range(3))
+        held[channel] = windows(fields.at[3], channel * blocks, blocks)
+        left = spread(
+            joined_parts(signal, single.at[channel, 0], -1), padded.at[channel, 0], -1
+        )
+        sums = jnp.dot(left, held[channel], preferred_element_type=jnp.float32)
+        conv = overlapped(sums[:, :LANES] + sums[:, LANES:], -1)
         mixed = gating * conv
         sigmoid_val = jax.nn.sigmoid(mixed)
-        back = gating * probing * sigmoid_val * (1.0 + mixed * (1.0 - sigmoid_val))
-        joined = joined_parts(back, single.at[channel, 2], 1)
-        high = [vals.astype(jnp.bfloat16).astype(jnp.float32) for vals in joined]
-        low = [vals - term for vals, term in zip(joined, high)]
-        left = jnp.concatenate(
-            [
-                spread(vals, padded.at[channel, 2 + term], 1)
-                for term, vals in enumerate((high, low))
-            ],
-            axis=0,
-        )
-
-        def filter_row(block, first=channel):
-            return taps_turned[block * SUBS + first : block * SUBS + first + 1, :]
-
-        right = windows(
-            filter_row, blocks, LANES + 1 - PART, lane_ids + PART - 1 - row_ids >= LANES
-        )
-        right = jnp.concatenate(
-            [jnp.concatenate(halves(rows), axis=1) for rows in right], axis=0
-        )
-        sums = jnp.dot(left, right, preferred_element_type=jnp.float32)
+        backs.append(gating * probing * sigmoid_val * (1.0 + mixed * (1.0 - sigmoid_val)))
+    cuts = (0, SUBS // 2, 3 * SUBS // 4, SUBS)
+    backs = jnp.concatenate(
+        [flipped(jnp.concatenate(backs[f:l], axis=0)) for f, l in zip(cuts, cuts[1:])], axis=0
+    )
+    for channel in range(SUBS):
+        place = slice(channel * blocks, (channel + 1) * blocks)
+        left = spread_terms(
+            joined_parts(backs[place], single.at[channel, 1], 1),
+            [padded.at[channel, 1 + term] for term in range(2)],
+            1,
+        )
+        sums = jnp.dot(left, held[channel], preferred_element_type=jnp.float32)
         sums = sums[:, :LANES] + sums[:, LANES:]
-        sums = sums[: PARTS * blocks] + sums[PARTS * blocks :]
-        grad = sums[(PARTS - 1) * blocks :]
-        for part in range(PARTS - 1):
-            own = sums[part * blocks : (part + 1) * blocks]
-            kept = lanes >= LANES - (part + 1) * PART
-            grad = grad + turn(jnp.where(kept, own, next_block(own, 1)), part + 1)
-        saliency = grad * signal
+        grad = overlapped(sums[: PARTS * blocks] + sums[PARTS * blocks :], 1)
+        saliency = grad * fields[4, place, :]
         position_sums += saliency
         products[place, :] = saliency
-    pick = iota((SUBS, LANES), 1) // BLOCK == iota((SUBS, LANES), 0)
+    position_sums = flipped(position_sums)
+    pick = (LANES - 1 - iota((SUBS, LANES), 1)) // BLOCK == iota((SUBS, LANES), 0)
     pick = pick.astype(jnp.float32).astype(jnp.bfloat16)
     block_sums = sum(
         lax.dot_general(
@@ -275,7 +272,7 @@
     )
     own = lax.axis_index("ch")
     for copy in range(copies):
-        rest = jnp.where(own == copy, block_sums[:2], members_ref[...])
+        rest = jnp.where(own == copy, block_sums[:2], members)
         for device in range(devices):
             sums_ref[copy * devices + device, :, :] = jnp.concatenate(
                 [position_sums[2 * device : 2 * device + 2], rest], axis=0
@@ -344,14 +341,14 @@
         member_nodes.reshape(1, -1),
         node_place.reshape(-1, LANES),
     )
-    packed, members = pl.pallas_call(
+    packed, *lists = pl.pallas_call(
         pack_kernel,
         out_shape=(
             jax.ShapeDtypeStruct((devices, PACK_ROWS, LANES), jnp.bfloat16),
-            jax.ShapeDtypeStruct((2, LANES), jnp.float32),
+            *(jax.ShapeDtypeStruct(part.shape, part.dtype) for part in local[4:]),
         ),
         in_specs=[pl.BlockSpec(memory_space=pltpu.HBM)] * len(local),
-        scratch_shapes=[pltpu.VMEM(part.shape, part.dtype) for part in local]
+        scratch_shapes=[pltpu.VMEM(part.shape, part.dtype) for part in local[:4]]
         + [pltpu.SemaphoreType.DMA((len(local),))],
         compiler_params=LEAN,
         name="pack",
@@ -362,14 +359,14 @@
         out_shape=jax.ShapeDtypeStruct((devices * copies, 4, LANES), jnp.float32),
         scratch_shapes=[
             pltpu.VMEM((FIELDS, SUBS * blocks, LANES), jnp.float32),
-            pltpu.VMEM((blocks * SUBS, LANES), jnp.float32),
-            pltpu.VMEM((SUBS, 3, 2 * blocks, LANES), jnp.float32),
-            pltpu.VMEM((SUBS, 4, PARTS, 2 * blocks, LANES), jnp.float32),
+            pltpu.VMEM((SUBS, 2, 2 * blocks, LANES), jnp.float32),
+            pltpu.VMEM((SUBS, 3, PARTS, 2 * blocks, LANES), jnp.float32),
             pltpu.VMEM((SUBS * blocks, LANES), jnp.float32),
+            pltpu.VMEM((SUBS, blocks * PART, 2 * LANES), jnp.bfloat16),
         ],
         compiler_params=LEAN,
         name="saliency",
-    )(packed, members)
+    )(packed, *lists)
     sums = lax.all_to_all(sums, ("ch", "seq"), split_axis=0, concat_axis=0, tiled=True)
     position, node_rows = pl.pallas_call(
         functools.partial(finish_kernel, devices * member_nodes.shape[0], channels * copies),
@@ -586,7 +583,8 @@
     devices = lax.axis_size("seq")
     members = args[4].shape[0]
     fits = channels == SUBS * devices and devices == SUBS and length == 2 * LANES
-    if fits and members == SUBS and NODES % (devices * LANES) == 0:
+    fits = fits and members == SUBS and lax.axis_size("ch") > 1
+    if fits and NODES % (devices * LANES) == 0:
         return whole_channels(*args)
     return spread_channels(*args)
 

time: 30 us -> 29.4 us (0.980)
  Pallas kernels: 4.54 us -> 3.91 us
    pallas_call x1, Pallas kernels: 2.28 us -> 1.84 us  [whole_channels(): pl.pallas_call(saliency_kernel, out_shape=jax.ShapeDtypeStruct((devices *...]
where the time goes in v4:
time: 29.4 us; the launch traced here: 29.1 us
  blocking collectives  24.6 us (84%)
  Pallas kernels  3.91 us (13%)
  between operations  0.65 us (2%)
    all_to_all x1, blocking collectives, whole_channels(): lax.all_to_all(packed, 'seq', split_axis=0, concat_axis=0, tiled=True)  14.6 us
    all_to_all x1, blocking collectives, whole_channels(): lax.all_to_all(sums, ('ch', 'seq'), split_axis=0, concat_axis=0, tiled=True)  9.94 us
    pallas_call x1, Pallas kernels, whole_channels(): pl.pallas_call(saliency_kernel, out_shape=jax.ShapeDtypeStruct((devices *...  1.84 us
    pallas_call x1, Pallas kernels, whole_channels(): pl.pallas_call(functools.partial(finish_kernel, devices * member_nodes.sh...  1.09 us
    pallas_call x1, Pallas kernels, whole_channels(): pl.pallas_call(pack_kernel, out_shape=(jax.ShapeDtypeStruct((devices, PAC...  0.98 us

profile of v4, /device:TPU:0, one launch (start us, length us, event | category | flops | bytes accessed | tf_op | source)
XLA Modules:
  0.0 29.1 jit_solution(12686745501463646285)
XLA Ops:
  0.6 1.0 %pack.1 = (bf16[8,80,128]{2,1,0:T(8,128)(2,1)S(1)}, s32[1,8]{1,0:T(1,128)S(1)}, s32[1,8]{1,0:T(1,128)S(1)}, s32[64,128]{1,0:T(8,128)S(1)}) custom-call(bf16[64,256]{1,0:T(8,128)(2,1)} %refs_0_.1, bf16[64,256]{1,0:T(8,128)(2,1)} %refs_1_.1, bf16[64,256]{1,0:T(8,128)(2,1)} %refs_2_.1, f32[64,256]{1,0:T(8,128)} %refs_3_.1, s32[1,8]{1,0:T(1,128)} %bitcast.5, ...), custom_call_target="tpu_custom_call" | custom-call | tf_op jit(solution)/shard_map/pack/pallas_call | solution.py:344
  1.6 14.6 %all_to_all.10.packed_ref = bf16[8,80,128]{2,1,0:T(8,128)(2,1)S(1)} all-to-all(bf16[8,80,128]{2,1,0:T(8,128)(2,1)S(1)} %get-tuple-element.8), channel_id=1, replica_groups=mesh['seq'=8,'ch'=4] {'seq'}, dimensions={0} | all-to-all | bytes 327680 | tf_op jit(solution)/shard_map/all_to_all | solution.py:356
  16.3 1.8 %saliency.1 = f32[32,4,128]{2,1,0:T(4,128)S(1)} custom-call(bf16[8,80,128]{2,1,0:T(8,128)(2,1)S(1)} %all_to_all.10.packed_ref, s32[1,8]{1,0:T(1,128)S(1)} %get-tuple-element.9.blocks_ref, s32[1,8]{1,0:T(1,128)S(1)} %get-tuple-element.10.nodes_ref, s32[64,128]{1,0:T(8,128)S(1)} %get-tuple-element.11.place_ref), custom_call_target="tpu_custom_call" | custom-call | tf_op jit(solution)/shard_map/saliency/pallas_call | solution.py:357
  18.1 9.9 %all_to_all.11.sums_ref = f32[32,4,128]{2,1,0:T(4,128)S(1)} all-to-all(f32[32,4,128]{2,1,0:T(4,128)S(1)} %saliency.1), channel_id=1, replica_groups=mesh['seq'=8,'ch'=4] {'ch','seq'}, dimensions={0} | all-to-all | bytes 131072 | tf_op jit(solution)/shard_map/all_to_all | solution.py:370
  28.0 1.1 %finish.1 = (f32[2,128]{1,0:T(2,128)}, f32[64,1024]{1,0:T(8,128)}) custom-call(f32[32,4,128]{2,1,0:T(4,128)S(1)} %all_to_all.11.sums_ref), custom_call_target="tpu_custom_call" | custom-call | tf_op jit(solution)/shard_map/finish/pallas_call | solution.py:371

commit v5 on v4

--- a/solution.py
+++ b/solution.py
@@ -119,31 +119,21 @@
     return pltpu.roll(vals, shift, axis=1) if shift else vals
 
 
-def exchanged(pieces):
-    lanes = iota(pieces[0].shape, 1)
-    low = lanes < 2 * PART
-    crossed = [None] * PARTS
-    for place in range(2):
-        first, second = pieces[place], pieces[place + 2]
-        swapped = turn(jnp.where(low, second, first), 2)
-        crossed[place] = jnp.where(low, first, swapped)
-        crossed[place + 2] = jnp.where(low, swapped, second)
-    even = lanes % (2 * PART) < PART
+def joined_parts(copies, single, sign):
+    blocks = copies.shape[0]
+    lanes = iota((blocks, LANES), 1)
+    start = blocks if sign < 0 else 0
     result = []
-    for first, second in (crossed[:2], crossed[2:]):
-        result.append(jnp.where(even, first, turn(second, 1)))
-        result.append(jnp.where(even, turn(first, -1), second))
+    for part in range(PARTS):
+        rows = single.at[part]
+        rows[start : start + blocks, :] = copies[:, part * LANES : (part + 1) * LANES]
+        rows[blocks - start : 2 * blocks - start, :] = jnp.zeros((blocks, LANES), jnp.float32)
+        joined = rows[start : start + blocks, :]
+        for step in range(1, PARTS):
+            moved = rows[start + sign * step : start + sign * step + blocks, :]
+            joined = jnp.where(lanes < step * PART, joined, moved)
+        result.append(joined)
     return result
-
-
-def joined_parts(rows, single, sign):
-    blocks = rows.shape[0]
-    start = blocks if sign < 0 else 0
-    single[start : start + blocks, :] = rows
-    single[blocks - start : 2 * blocks - start, :] = jnp.zeros((blocks, LANES), jnp.float32)
-    return exchanged(
-        [single[start + sign * step : start + sign * step + blocks, :] for step in range(PARTS)]
-    )
 
 
 def spread(joined, padded, sign):
@@ -219,13 +209,23 @@
                 fields[field, place, :] = rows[field][side * SUBS : (side + 1) * SUBS]
     flip = iota((LANES, LANES), 0) + iota((LANES, LANES), 1) == LANES - 1
     flip = flip.astype(jnp.float32).astype(jnp.bfloat16)
-    flip_both = jnp.concatenate([flip, flip], axis=0)
-
-    def flipped(vals):
+    lane_ids, column_ids = (iota((LANES, PARTS * LANES), dim) for dim in range(2))
+    origins = column_ids // LANES * PART + column_ids % PART
+    repeat, flip_repeat = (
+        (ids == origins).astype(jnp.float32).astype(jnp.bfloat16)
+        for ids in (lane_ids, LANES - 1 - lane_ids)
+    )
+
+    def both_terms(vals, chosen):
         return jnp.dot(
-            jnp.concatenate(halves(vals), axis=1), flip_both, preferred_element_type=jnp.float32
-        )
-
+            jnp.concatenate(halves(vals), axis=1),
+            jnp.concatenate([chosen, chosen], axis=0),
+            preferred_element_type=jnp.float32,
+        )
+
+    signals = jnp.dot(
+        fields[0].astype(jnp.bfloat16), repeat, preferred_element_type=jnp.float32
+    )
     fields[4] = jnp.dot(
         fields[0].astype(jnp.bfloat16), flip, preferred_element_type=jnp.float32
     )
@@ -234,10 +234,10 @@
     backs = []
     for channel in range(SUBS):
         place = slice(channel * blocks, (channel + 1) * blocks)
-        signal, gating, probing = (fields[field, place, :] for field in range(3))
+        gating, probing = fields[1, place, :], fields[2, place, :]
         held[channel] = windows(fields.at[3], channel * blocks, blocks)
         left = spread(
-            joined_parts(signal, single.at[channel, 0], -1), padded.at[channel, 0], -1
+            joined_parts(signals[place], single.at[channel, 0], -1), padded.at[channel, 0], -1
         )
         sums = jnp.dot(left, held[channel], preferred_element_type=jnp.float32)
         conv = overlapped(sums[:, :LANES] + sums[:, LANES:], -1)
@@ -246,7 +246,11 @@
         backs.append(gating * probing * sigmoid_val * (1.0 + mixed * (1.0 - sigmoid_val)))
     cuts = (0, SUBS // 2, 3 * SUBS // 4, SUBS)
     backs = jnp.concatenate(
-        [flipped(jnp.concatenate(backs[f:l], axis=0)) for f, l in zip(cuts, cuts[1:])], axis=0
+        [
+            both_terms(jnp.concatenate(backs[f:l], axis=0), flip_repeat)
+            for f, l in zip(cuts, cuts[1:])
+        ],
+        axis=0,
     )
     for channel in range(SUBS):
         place = slice(channel * blocks, (channel + 1) * blocks)
@@ -261,7 +265,7 @@
         saliency = grad * fields[4, place, :]
         position_sums += saliency
         products[place, :] = saliency
-    position_sums = flipped(position_sums)
+    position_sums = both_terms(position_sums, flip)
     pick = (LANES - 1 - iota((SUBS, LANES), 1)) // BLOCK == iota((SUBS, LANES), 0)
     pick = pick.astype(jnp.float32).astype(jnp.bfloat16)
     block_sums = sum(
@@ -359,7 +363,7 @@
         out_shape=jax.ShapeDtypeStruct((devices * copies, 4, LANES), jnp.float32),
         scratch_shapes=[
             pltpu.VMEM((FIELDS, SUBS * blocks, LANES), jnp.float32),
-            pltpu.VMEM((SUBS, 2, 2 * blocks, LANES), jnp.float32),
+            pltpu.VMEM((SUBS, 2, PARTS, 2 * blocks, LANES), jnp.float32),
             pltpu.VMEM((SUBS, 3, PARTS, 2 * blocks, LANES), jnp.float32),
             pltpu.VMEM((SUBS * blocks, LANES), jnp.float32),
             pltpu.VMEM((SUBS, blocks * PART, 2 * LANES), jnp.bfloat16),

time: 29.4 us -> 29.2 us (level)
  no operation moved by 1% of the time
where the time goes in v5:
time: 29.2 us; the launch traced here: 29 us
  blocking collectives  24.6 us (84%)
  Pallas kernels  3.81 us (13%)
  between operations  0.65 us (2%)
    all_to_all x1, blocking collectives, whole_channels(): lax.all_to_all(packed, 'seq', split_axis=0, concat_axis=0, tiled=True)  14.6 us
    all_to_all x1, blocking collectives, whole_channels(): lax.all_to_all(sums, ('ch', 'seq'), split_axis=0, concat_axis=0, tiled=True)  9.92 us
    pallas_call x1, Pallas kernels, whole_channels(): pl.pallas_call(saliency_kernel, out_shape=jax.ShapeDtypeStruct((devices *...  1.75 us
    pallas_call x1, Pallas kernels, whole_channels(): pl.pallas_call(functools.partial(finish_kernel, devices * member_nodes.sh...  1.09 us
    pallas_call x1, Pallas kernels, whole_channels(): pl.pallas_call(pack_kernel, out_shape=(jax.ShapeDtypeStruct((devices, PAC...  0.98 us

profile of v5, /device:TPU:0, one launch (start us, length us, event | category | flops | bytes accessed | tf_op | source)
XLA Modules:
  0.0 29.0 jit_solution(4018625785393856403)
XLA Ops:
  0.6 1.0 %pack.1 = (bf16[8,80,128]{2,1,0:T(8,128)(2,1)S(1)}, s32[1,8]{1,0:T(1,128)S(1)}, s32[1,8]{1,0:T(1,128)S(1)}, s32[64,128]{1,0:T(8,128)S(1)}) custom-call(bf16[64,256]{1,0:T(8,128)(2,1)} %refs_0_.1, bf16[64,256]{1,0:T(8,128)(2,1)} %refs_1_.1, bf16[64,256]{1,0:T(8,128)(2,1)} %refs_2_.1, f32[64,256]{1,0:T(8,128)} %refs_3_.1, s32[1,8]{1,0:T(1,128)} %bitcast.5, ...), custom_call_target="tpu_custom_call" | custom-call | tf_op jit(solution)/shard_map/pack/pallas_call | solution.py:348
  1.6 14.6 %all_to_all.10.packed_ref = bf16[8,80,128]{2,1,0:T(8,128)(2,1)S(1)} all-to-all(bf16[8,80,128]{2,1,0:T(8,128)(2,1)S(1)} %get-tuple-element.8), channel_id=1, replica_groups=mesh['seq'=8,'ch'=4] {'seq'}, dimensions={0} | all-to-all | bytes 327680 | tf_op jit(solution)/shard_map/all_to_all | solution.py:360
  16.3 1.7 %saliency.1 = f32[32,4,128]{2,1,0:T(4,128)S(1)} custom-call(bf16[8,80,128]{2,1,0:T(8,128)(2,1)S(1)} %all_to_all.10.packed_ref, s32[1,8]{1,0:T(1,128)S(1)} %get-tuple-element.9.blocks_ref, s32[1,8]{1,0:T(1,128)S(1)} %get-tuple-element.10.nodes_ref, s32[64,128]{1,0:T(8,128)S(1)} %get-tuple-element.11.place_ref), custom_call_target="tpu_custom_call" | custom-call | tf_op jit(solution)/shard_map/saliency/pallas_call | solution.py:361
  18.0 9.9 %all_to_all.11.sums_ref = f32[32,4,128]{2,1,0:T(4,128)S(1)} all-to-all(f32[32,4,128]{2,1,0:T(4,128)S(1)} %saliency.1), channel_id=1, replica_groups=mesh['seq'=8,'ch'=4] {'ch','seq'}, dimensions={0} | all-to-all | bytes 131072 | tf_op jit(solution)/shard_map/all_to_all | solution.py:374
  27.9 1.1 %finish.1 = (f32[2,128]{1,0:T(2,128)}, f32[64,1024]{1,0:T(8,128)}) custom-call(f32[32,4,128]{2,1,0:T(4,128)S(1)} %all_to_all.11.sums_ref), custom_call_target="tpu_custom_call" | custom-call | tf_op jit(solution)/shard_map/finish/pallas_call | solution.py:375

commit v6 on v5

--- a/solution.py
+++ b/solution.py
@@ -31,6 +31,10 @@
 def halves(vals):
     high = vals.astype(jnp.bfloat16)
     return high, (vals - high.astype(jnp.float32)).astype(jnp.bfloat16)
+
+
+def exchange_order(devices):
+    return [(place + devices // 2 + 1) % devices for place in range(devices)]
 
 
 def as_column(row, count):
@@ -77,13 +81,14 @@
     ]
     for load in loads:
         load.start()
+    order = exchange_order(packed_ref.shape[0])
 
     def put(pair, field, tiles):
         for side in range(2):
             rows = slice(side * SUBS, (side + 1) * SUBS)
             both = jnp.concatenate([tile[rows] for tile in tiles], axis=0)
             place = slice(field * FIELD_ROWS, (field + 1) * FIELD_ROWS)
-            packed_ref[2 * pair + side, place, :] = both.astype(jnp.bfloat16)
+            packed_ref[order.index(2 * pair + side), place, :] = both.astype(jnp.bfloat16)
 
     columns = [slice(0, LANES), slice(LANES, 2 * LANES)]
     for field in range(4):
@@ -197,9 +202,9 @@
     devices = packed_ref.shape[0]
     blocks = 2 * devices
     copies = sums_ref.shape[0] // devices
-    for source in range(devices):
+    for slot, source in enumerate(exchange_order(devices)):
         rows = [
-            packed_ref[source, field * FIELD_ROWS : (field + 1) * FIELD_ROWS, :].astype(jnp.float32)
+            packed_ref[slot, field * FIELD_ROWS : (field + 1) * FIELD_ROWS, :].astype(jnp.float32)
             for field in range(FIELDS)
         ]
         rows = [*rows[:3], rows[3] + rows[4]]
@@ -357,7 +362,14 @@
         compiler_params=LEAN,
         name="pack",
     )(*(pltpu.with_memory_space_constraint(part, pltpu.HBM) for part in local))
-    packed = lax.all_to_all(packed, "seq", split_axis=0, concat_axis=0, tiled=True)
+    packed = lax.all_to_all(
+        packed,
+        "seq",
+        split_axis=0,
+        concat_axis=0,
+        tiled=True,
+        axis_index_groups=[exchange_order(devices)],
+    )
     sums = pl.pallas_call(
         saliency_kernel,
         out_shape=jax.ShapeDtypeStruct((devices * copies, 4, LANES), jnp.float32),

time: 29.2 us -> 28 us (0.959)
  blocking collectives: 24.6 us -> 23.3 us
    all_to_all x1, blocking collectives: 14.6 us -> 12.4 us  [whole_channels(): lax.all_to_all(packed, 'seq', split_axis=0, concat_axis=0, tiled=True, ax...]
    all_to_all x1, blocking collectives: 9.92 us -> 10.9 us  [whole_channels(): lax.all_to_all(sums, ('ch', 'seq'), split_axis=0, concat_axis=0, tiled=True)]
where the time goes in v6:
time: 28 us; the launch traced here: 27.8 us
  blocking collectives  23.3 us (83%)
  Pallas kernels  3.82 us (14%)
  between operations  0.65 us (2%)
    all_to_all x1, blocking collectives, whole_channels(): lax.all_to_all(packed, 'seq', split_axis=0, concat_axis=0, tiled=True, ax...  12.4 us
    all_to_all x1, blocking collectives, whole_channels(): lax.all_to_all(sums, ('ch', 'seq'), split_axis=0, concat_axis=0, tiled=True)  10.9 us
    pallas_call x1, Pallas kernels, whole_channels(): pl.pallas_call(saliency_kernel, out_shape=jax.ShapeDtypeStruct((devices *...  1.76 us
    pallas_call x1, Pallas kernels, whole_channels(): pl.pallas_call(functools.partial(finish_kernel, devices * member_nodes.sh...  1.09 us
    pallas_call x1, Pallas kernels, whole_channels(): pl.pallas_call(pack_kernel, out_shape=(jax.ShapeDtypeStruct((devices, PAC...  0.98 us

profile of v6, /device:TPU:0, one launch (start us, length us, event | category | flops | bytes accessed | tf_op | source)
XLA Modules:
  0.0 27.8 jit_solution(10398864369136051244)
XLA Ops:
  0.6 1.0 %pack.1 = (bf16[8,80,128]{2,1,0:T(8,128)(2,1)S(1)}, s32[1,8]{1,0:T(1,128)S(1)}, s32[1,8]{1,0:T(1,128)S(1)}, s32[64,128]{1,0:T(8,128)S(1)}) custom-call(bf16[64,256]{1,0:T(8,128)(2,1)} %refs_0_.1, bf16[64,256]{1,0:T(8,128)(2,1)} %refs_1_.1, bf16[64,256]{1,0:T(8,128)(2,1)} %refs_2_.1, f32[64,256]{1,0:T(8,128)} %refs_3_.1, s32[1,8]{1,0:T(1,128)} %bitcast.5, ...), custom_call_target="tpu_custom_call" | custom-call | tf_op jit(solution)/shard_map/pack/pallas_call | solution.py:353
  1.6 12.4 %all_to_all.10.packed_ref = bf16[8,80,128]{2,1,0:T(8,128)(2,1)S(1)} all-to-all(bf16[8,80,128]{2,1,0:T(8,128)(2,1)S(1)} %get-tuple-element.8), channel_id=1, replica_groups={{20,24,28,0,4,8,12,16},{21,25,29,1,5,9,13,17},{22,26,30,2,6,10,14,18},{..., dimensions={0} | all-to-all | bytes 327680 | tf_op jit(solution)/shard_map/all_to_all | solution.py:365
  14.0 1.8 %saliency.1 = f32[32,4,128]{2,1,0:T(4,128)S(1)} custom-call(bf16[8,80,128]{2,1,0:T(8,128)(2,1)S(1)} %all_to_all.10.packed_ref, s32[1,8]{1,0:T(1,128)S(1)} %get-tuple-element.9.blocks_ref, s32[1,8]{1,0:T(1,128)S(1)} %get-tuple-element.10.nodes_ref, s32[64,128]{1,0:T(8,128)S(1)} %get-tuple-element.11.place_ref), custom_call_target="tpu_custom_call" | custom-call | tf_op jit(solution)/shard_map/saliency/pallas_call | solution.py:373
  15.7 10.9 %all_to_all.11.sums_ref = f32[32,4,128]{2,1,0:T(4,128)S(1)} all-to-all(f32[32,4,128]{2,1,0:T(4,128)S(1)} %saliency.1), channel_id=1, replica_groups=mesh['seq'=8,'ch'=4] {'ch','seq'}, dimensions={0} | all-to-all | bytes 131072 | tf_op jit(solution)/shard_map/all_to_all | solution.py:386
  26.7 1.1 %finish.1 = (f32[2,128]{1,0:T(2,128)}, f32[64,1024]{1,0:T(8,128)}) custom-call(f32[32,4,128]{2,1,0:T(4,128)S(1)} %all_to_all.11.sums_ref), custom_call_target="tpu_custom_call" | custom-call | tf_op jit(solution)/shard_map/finish/pallas_call | solution.py:387

commit v7 on v6

--- a/solution.py
+++ b/solution.py
@@ -34,7 +34,9 @@
 
 
 def exchange_order(devices):
-    return [(place + devices // 2 + 1) % devices for place in range(devices)]
+    listed = [*range(0, devices, 2), *range(1, devices, 2)]
+    first = devices // 2 - 1
+    return listed[first:] + listed[:first]
 
 
 def as_column(row, count):

time: 28 us -> 27.6 us (0.986)
  blocking collectives: 23.3 us -> 22.9 us
    all_to_all x1, blocking collectives: 10.9 us -> 9.91 us  [whole_channels(): lax.all_to_all(sums, ('ch', 'seq'), split_axis=0, concat_axis=0, tiled=True)]
    all_to_all x1, blocking collectives: 12.4 us -> 13 us  [whole_channels(): lax.all_to_all(packed, 'seq', split_axis=0, concat_axis=0, tiled=True, ax...]
where the time goes in v7:
time: 27.6 us; the launch traced here: 27.4 us
  blocking collectives  22.9 us (83%)
  Pallas kernels  3.82 us (14%)
  between operations  0.65 us (2%)
    all_to_all x1, blocking collectives, whole_channels(): lax.all_to_all(packed, 'seq', split_axis=0, concat_axis=0, tiled=True, ax...  13 us
    all_to_all x1, blocking collectives, whole_channels(): lax.all_to_all(sums, ('ch', 'seq'), split_axis=0, concat_axis=0, tiled=True)  9.91 us
    pallas_call x1, Pallas kernels, whole_channels(): pl.pallas_call(saliency_kernel, out_shape=jax.ShapeDtypeStruct((devices *...  1.75 us
    pallas_call x1, Pallas kernels, whole_channels(): pl.pallas_call(functools.partial(finish_kernel, devices * member_nodes.sh...  1.09 us
    pallas_call x1, Pallas kernels, whole_channels(): pl.pallas_call(pack_kernel, out_shape=(jax.ShapeDtypeStruct((devices, PAC...  0.98 us

profile of v7, /device:TPU:0, one launch (start us, length us, event | category | flops | bytes accessed | tf_op | source)
XLA Modules:
  0.0 27.4 jit_solution(7552731840062037891)
XLA Ops:
  0.6 1.0 %pack.1 = (bf16[8,80,128]{2,1,0:T(8,128)(2,1)S(1)}, s32[1,8]{1,0:T(1,128)S(1)}, s32[1,8]{1,0:T(1,128)S(1)}, s32[64,128]{1,0:T(8,128)S(1)}) custom-call(bf16[64,256]{1,0:T(8,128)(2,1)} %refs_0_.1, bf16[64,256]{1,0:T(8,128)(2,1)} %refs_1_.1, bf16[64,256]{1,0:T(8,128)(2,1)} %refs_2_.1, f32[64,256]{1,0:T(8,128)} %refs_3_.1, s32[1,8]{1,0:T(1,128)} %bitcast.5, ...), custom_call_target="tpu_custom_call" | custom-call | tf_op jit(solution)/shard_map/pack/pallas_call | solution.py:355
  1.6 13.0 %all_to_all.10.packed_ref = bf16[8,80,128]{2,1,0:T(8,128)(2,1)S(1)} all-to-all(bf16[8,80,128]{2,1,0:T(8,128)(2,1)S(1)} %get-tuple-element.8), channel_id=1, replica_groups={{24,4,12,20,28,0,8,16},{25,5,13,21,29,1,9,17},{26,6,14,22,30,2,10,18},{..., dimensions={0} | all-to-all | bytes 327680 | tf_op jit(solution)/shard_map/all_to_all | solution.py:367
  14.6 1.8 %saliency.1 = f32[32,4,128]{2,1,0:T(4,128)S(1)} custom-call(bf16[8,80,128]{2,1,0:T(8,128)(2,1)S(1)} %all_to_all.10.packed_ref, s32[1,8]{1,0:T(1,128)S(1)} %get-tuple-element.9.blocks_ref, s32[1,8]{1,0:T(1,128)S(1)} %get-tuple-element.10.nodes_ref, s32[64,128]{1,0:T(8,128)S(1)} %get-tuple-element.11.place_ref), custom_call_target="tpu_custom_call" | custom-call | tf_op jit(solution)/shard_map/saliency/pallas_call | solution.py:375
  16.4 9.9 %all_to_all.11.sums_ref = f32[32,4,128]{2,1,0:T(4,128)S(1)} all-to-all(f32[32,4,128]{2,1,0:T(4,128)S(1)} %saliency.1), channel_id=1, replica_groups=mesh['seq'=8,'ch'=4] {'ch','seq'}, dimensions={0} | all-to-all | bytes 131072 | tf_op jit(solution)/shard_map/all_to_all | solution.py:388
  26.3 1.1 %finish.1 = (f32[2,128]{1,0:T(2,128)}, f32[64,1024]{1,0:T(8,128)}) custom-call(f32[32,4,128]{2,1,0:T(4,128)S(1)} %all_to_all.11.sums_ref), custom_call_target="tpu_custom_call" | custom-call | tf_op jit(solution)/shard_map/finish/pallas_call | solution.py:389

commit v8 on v7

--- a/solution.py
+++ b/solution.py
@@ -34,8 +34,8 @@
 
 
 def exchange_order(devices):
-    listed = [*range(0, devices, 2), *range(1, devices, 2)]
-    first = devices // 2 - 1
+    listed = [*range(1, devices, 2), *range(0, devices, 2)]
+    first = devices // 4
     return listed[first:] + listed[:first]
 
 

time: 27.6 us -> 27.5 us (level)
    all_to_all x1, blocking collectives: 13 us -> 12.3 us  [whole_channels(): lax.all_to_all(packed, 'seq', split_axis=0, concat_axis=0, tiled=True, ax...]
    all_to_all x1, blocking collectives: 9.91 us -> 10.5 us  [whole_channels(): lax.all_to_all(sums, ('ch', 'seq'), split_axis=0, concat_axis=0, tiled=True)]
where the time goes in v8:
time: 27.5 us; the launch traced here: 27.3 us
  blocking collectives  22.8 us (83%)
  Pallas kernels  3.82 us (14%)
  between operations  0.65 us (2%)
    all_to_all x1, blocking collectives, whole_channels(): lax.all_to_all(packed, 'seq', split_axis=0, concat_axis=0, tiled=True, ax...  12.3 us
    all_to_all x1, blocking collectives, whole_channels(): lax.all_to_all(sums, ('ch', 'seq'), split_axis=0, concat_axis=0, tiled=True)  10.5 us
    pallas_call x1, Pallas kernels, whole_channels(): pl.pallas_call(saliency_kernel, out_shape=jax.ShapeDtypeStruct((devices *...  1.76 us
    pallas_call x1, Pallas kernels, whole_channels(): pl.pallas_call(functools.partial(finish_kernel, devices * member_nodes.sh...  1.09 us
    pallas_call x1, Pallas kernels, whole_channels(): pl.pallas_call(pack_kernel, out_shape=(jax.ShapeDtypeStruct((devices, PAC...  0.98 us

profile of v8, /device:TPU:0, one launch (start us, length us, event | category | flops | bytes accessed | tf_op | source)
XLA Modules:
  0.0 27.3 jit_solution(3698406171892351696)
XLA Ops:
  0.6 1.0 %pack.1 = (bf16[8,80,128]{2,1,0:T(8,128)(2,1)S(1)}, s32[1,8]{1,0:T(1,128)S(1)}, s32[1,8]{1,0:T(1,128)S(1)}, s32[64,128]{1,0:T(8,128)S(1)}) custom-call(bf16[64,256]{1,0:T(8,128)(2,1)} %refs_0_.1, bf16[64,256]{1,0:T(8,128)(2,1)} %refs_1_.1, bf16[64,256]{1,0:T(8,128)(2,1)} %refs_2_.1, f32[64,256]{1,0:T(8,128)} %refs_3_.1, s32[1,8]{1,0:T(1,128)} %bitcast.5, ...), custom_call_target="tpu_custom_call" | custom-call | tf_op jit(solution)/shard_map/pack/pallas_call | solution.py:355
  1.6 12.3 %all_to_all.10.packed_ref = bf16[8,80,128]{2,1,0:T(8,128)(2,1)S(1)} all-to-all(bf16[8,80,128]{2,1,0:T(8,128)(2,1)S(1)} %get-tuple-element.8), channel_id=1, replica_groups={{20,28,0,8,16,24,4,12},{21,29,1,9,17,25,5,13},{22,30,2,10,18,26,6,14},{..., dimensions={0} | all-to-all | bytes 327680 | tf_op jit(solution)/shard_map/all_to_all | solution.py:367
  13.9 1.8 %saliency.1 = f32[32,4,128]{2,1,0:T(4,128)S(1)} custom-call(bf16[8,80,128]{2,1,0:T(8,128)(2,1)S(1)} %all_to_all.10.packed_ref, s32[1,8]{1,0:T(1,128)S(1)} %get-tuple-element.9.blocks_ref, s32[1,8]{1,0:T(1,128)S(1)} %get-tuple-element.10.nodes_ref, s32[64,128]{1,0:T(8,128)S(1)} %get-tuple-element.11.place_ref), custom_call_target="tpu_custom_call" | custom-call | tf_op jit(solution)/shard_map/saliency/pallas_call | solution.py:375
  15.7 10.5 %all_to_all.11.sums_ref = f32[32,4,128]{2,1,0:T(4,128)S(1)} all-to-all(f32[32,4,128]{2,1,0:T(4,128)S(1)} %saliency.1), channel_id=1, replica_groups=mesh['seq'=8,'ch'=4] {'ch','seq'}, dimensions={0} | all-to-all | bytes 131072 | tf_op jit(solution)/shard_map/all_to_all | solution.py:388
  26.2 1.1 %finish.1 = (f32[2,128]{1,0:T(2,128)}, f32[64,1024]{1,0:T(8,128)}) custom-call(f32[32,4,128]{2,1,0:T(4,128)S(1)} %all_to_all.11.sums_ref), custom_call_target="tpu_custom_call" | custom-call | tf_op jit(solution)/shard_map/finish/pallas_call | solution.py:389
